TPU v7x, 256 devices: a whole 4x4x8 slice. The times are simulated.
256 devices in a mesh: section: 16 (over z, x_hi), dp: 16 (over y, x_lo, core).
Axes of the slice: x: 4 (x_hi: 2, x_lo: 2; x = x_hi * 2 + x_lo), y: 4, z: 8, core: 2. Of those that a mesh axis runs over, the one named last changes fastest.
Arguments:
- down_input: bfloat16 [2, 1024, 1024], P(None, 'dp')
- up_input: bfloat16 [2, 1024, 1024], P(None, 'dp')
- down_cot: bfloat16 [2, 1024, 1024], P(None, 'dp'), may hold values from -0.059814453 to 0.059814453
- up_cot: bfloat16 [2, 1024, 1024], P(None, 'dp'), may hold values from -0.059814453 to 0.059814453
- weight: bfloat16 [16, 1024, 1024], P('section', 'dp'), may hold values from -0.1875 to 0.1875
- gain: bfloat16 [16, 1024], P('section', 'dp'), may hold values from 0.5 to 2
Outputs:
- grad_weight: float32 [16, 1024, 1024], P('section', 'dp')
- grad_gain: float32 [16, 1024], P('section', 'dp')
All inputs are finite; a program needn't handle non-finite values.
Results may differ from a plain program's by a relative error of at most 0.035.
Values may be sent and summed in bfloat16 or wider, within the bound.
A program may use at most 64 MiB of HBM per device.

v0:
```python
import math

import jax
import jax.numpy as jnp
from jax import lax
from jax.sharding import PartitionSpec as P

EPSILON = 1e-05
CUBIC = 0.044715
SLOPE = math.sqrt(2.0 / math.pi)


def passed_along(block, axis, distance):
    devices = range(lax.axis_size(axis))
    route = [(i - distance, i) for i in devices if i - distance in devices]
    return lax.ppermute(block, axis, route)


def from_partner(x, axis, stride):
    return lax.ppermute(x, axis, [(i, i ^ 1 << stride) for i in range(lax.axis_size(axis))])


def gelu_pair(projected):
    argument = SLOPE * (projected + CUBIC * projected * projected * projected)
    tangent = jnp.tanh(argument)
    gelu_value = 0.5 * projected * (1.0 + tangent)
    gelu_slope = 0.5 * (1.0 + tangent) + 0.5 * projected * (1.0 - tangent * tangent) * SLOPE * (
        1.0 + 3.0 * CUBIC * projected * projected
    )
    return (gelu_value, gelu_slope)


def layer_forward(layer_input, gain_row, weight_matrix):
    widened = layer_input.astype(jnp.float32)
    inverse = lax.rsqrt(jnp.mean(widened * widened, axis=-1, keepdims=True) + EPSILON)
    normed = (widened * inverse * gain_row.astype(jnp.float32)).astype(jnp.bfloat16)
    projected = jnp.dot(normed, weight_matrix, preferred_element_type=jnp.float32)
    gelu_value, _ = gelu_pair(projected)
    return ((widened + gelu_value).astype(jnp.bfloat16), normed, projected, inverse)


def layer_backward(cot_rows, layer_input, normed, projected, inverse, gain_row, weight_matrix):
    _, gelu_slope = gelu_pair(projected)
    grad_proj = (cot_rows.astype(jnp.float32) * gelu_slope).astype(jnp.bfloat16)
    weight_term = lax.dot_general(
        normed, grad_proj, (((0,), (0,)), ((), ())), preferred_element_type=jnp.float32
    )
    grad_normed = lax.dot_general(
        grad_proj, weight_matrix, (((1,), (1,)), ((), ())), preferred_element_type=jnp.float32
    )
    widened = layer_input.astype(jnp.float32)
    gain_term = jnp.sum(grad_normed * widened * inverse, axis=0)
    scaled_grad = gain_row.astype(jnp.float32) * grad_normed
    grad_input = inverse * scaled_grad - widened * inverse * inverse * inverse * jnp.mean(
        scaled_grad * widened, axis=-1, keepdims=True
    )
    return (
        (cot_rows.astype(jnp.float32) + grad_input).astype(jnp.bfloat16),
        weight_term,
        gain_term,
    )


def send_down_forward(rows_out):
    return passed_along(rows_out, "section", 1)


def send_up_forward(rows_out):
    return passed_along(rows_out, "section", -1)


def send_down_backward(rows_out):
    return passed_along(rows_out, "section", -1)


def send_up_backward(rows_out):
    return passed_along(rows_out, "section", 1)


def forward_turn(
    counter, received, saved_rows, inputs_all, position, weight_matrix, gain_row, sender
):
    batches = inputs_all.shape[0]
    batch_index = counter - position
    active = jnp.logical_and(batch_index >= 0, batch_index < batches)
    batch_slot = jnp.clip(batch_index, 0, batches - 1)
    layer_input = jnp.where(
        position == 0, lax.dynamic_index_in_dim(inputs_all, batch_slot, 0, False), received
    )

    def compute_layer(saved_now):
        output_rows, normed, projected, inverse = layer_forward(
            layer_input, gain_row, weight_matrix
        )
        pieces = (layer_input, normed, projected, inverse)
        updated = tuple(
            (
                lax.dynamic_update_index_in_dim(stored, piece, batch_slot, 0)
                for stored, piece in zip(saved_now, pieces)
            )
        )
        return (output_rows, updated)

    def forward_pass_through(saved_now):
        return (jnp.zeros_like(layer_input), saved_now)

    output_rows, saved_rows = lax.cond(active, compute_layer, forward_pass_through, saved_rows)
    return (sender(output_rows), saved_rows)


def backward_turn(
    counter, received, running, cots_all, position, saved_rows, weight_matrix, gain_row, sender
):
    batches = cots_all.shape[0]
    batch_index = counter - position
    active = jnp.logical_and(batch_index >= 0, batch_index < batches)
    batch_slot = jnp.clip(batch_index, 0, batches - 1)
    cot_rows = jnp.where(
        position == 0, lax.dynamic_index_in_dim(cots_all, batch_slot, 0, False), received
    )

    def compute_grads(running_now):
        stored = tuple(
            (lax.dynamic_index_in_dim(saved, batch_slot, 0, False) for saved in saved_rows)
        )
        earlier, weight_term, gain_term = layer_backward(
            cot_rows, stored[0], stored[1], stored[2], stored[3], gain_row, weight_matrix
        )
        return (earlier, (running_now[0] + weight_term, running_now[1] + gain_term))

    def backward_pass_through(running_now):
        return (jnp.zeros_like(cot_rows), running_now)

    earlier, running = lax.cond(active, compute_grads, backward_pass_through, running)
    return (sender(earlier), running)


def shards(down_input, up_input, down_cot, up_cot, weight, gain):
    sections = lax.axis_size("section")
    position = lax.axis_index("section")
    bit_count = sections.bit_length() - 1
    batches = down_input.shape[0]
    row_count = down_input.shape[1]
    width = down_input.shape[2]
    turns = sections + batches - 1
    mirror_weight, mirror_gain = (weight, gain)
    for bit_number in range(bit_count):
        mirror_weight, mirror_gain = from_partner(
            (mirror_weight, mirror_gain), "section", bit_number
        )
    own_weight, own_gain, far_weight, far_gain = (
        lax.all_gather(weight, "dp", axis=1, tiled=True),
        lax.all_gather(gain, "dp", axis=1, tiled=True),
        lax.all_gather(mirror_weight, "dp", axis=1, tiled=True),
        lax.all_gather(mirror_gain, "dp", axis=1, tiled=True),
    )
    own_weight, own_gain, far_weight, far_gain = (
        own_weight[0],
        own_gain[0],
        far_weight[0],
        far_gain[0],
    )
    up_place = sections - 1 - position
    empty_rows = jnp.zeros((row_count, width), jnp.bfloat16)
    empty_saved = (
        jnp.zeros((batches, row_count, width), jnp.bfloat16),
        jnp.zeros((batches, row_count, width), jnp.bfloat16),
        jnp.zeros((batches, row_count, width), jnp.float32),
        jnp.zeros((batches, row_count, 1), jnp.float32),
    )
    empty_grads = (jnp.zeros((width, width), jnp.float32), jnp.zeros((width,), jnp.float32))
    counters = jnp.arange(turns, dtype=jnp.int32)

    def down_forward_step(carry, counter):
        got_rows, saved_now = carry
        return (
            forward_turn(
                counter,
                got_rows,
                saved_now,
                down_input,
                position,
                own_weight,
                own_gain,
                send_down_forward,
            ),
            None,
        )

    def up_forward_step(carry, counter):
        got_rows, saved_now = carry
        return (
            forward_turn(
                counter,
                got_rows,
                saved_now,
                up_input,
                up_place,
                far_weight,
                far_gain,
                send_up_forward,
            ),
            None,
        )

    def down_backward_step(carry, counter):
        got_rows, running = carry
        return (
            backward_turn(
                counter,
                got_rows,
                running,
                down_cot,
                up_place,
                saved_down,
                own_weight,
                own_gain,
                send_down_backward,
            ),
            None,
        )

    def up_backward_step(carry, counter):
        got_rows, running = carry
        return (
            backward_turn(
                counter,
                got_rows,
                running,
                up_cot,
                position,
                saved_up,
                far_weight,
                far_gain,
                send_up_backward,
            ),
            None,
        )

    (_, saved_down), _ = lax.scan(down_forward_step, (empty_rows, empty_saved), counters)
    (_, saved_up), _ = lax.scan(up_forward_step, (empty_rows, empty_saved), counters)
    (_, grads_own), _ = lax.scan(down_backward_step, (empty_rows, empty_grads), counters)
    (_, grads_far), _ = lax.scan(up_backward_step, (empty_rows, empty_grads), counters)
    own_rows, own_gain_rows, far_rows, far_gain_rows = (
        lax.psum_scatter(
            grads_own[0].astype(jnp.bfloat16), "dp", scatter_dimension=0, tiled=True
        ).astype(jnp.float32),
        lax.psum_scatter(
            grads_own[1].astype(jnp.bfloat16), "dp", scatter_dimension=0, tiled=True
        ).astype(jnp.float32),
        lax.psum_scatter(
            grads_far[0].astype(jnp.bfloat16), "dp", scatter_dimension=0, tiled=True
        ).astype(jnp.float32),
        lax.psum_scatter(
            grads_far[1].astype(jnp.bfloat16), "dp", scatter_dimension=0, tiled=True
        ).astype(jnp.float32),
    )
    for bit_number in range(bit_count):
        far_rows, far_gain_rows = (
            from_partner(far_rows.astype(jnp.bfloat16), "section", bit_number).astype(
                far_rows.dtype
            ),
            from_partner(far_gain_rows.astype(jnp.bfloat16), "section", bit_number).astype(
                far_gain_rows.dtype
            ),
        )
    weight_rows = own_rows + far_rows
    gain_rows = own_gain_rows + far_gain_rows
    return (weight_rows[None], gain_rows[None])


def solution(mesh):
    placed = (
        P(None, "dp", None),
        P(None, "dp", None),
        P(None, "dp", None),
        P(None, "dp", None),
        P("section", "dp", None),
        P("section", "dp"),
    )
    return jax.shard_map(
        shards,
        mesh=mesh,
        in_specs=placed,
        out_specs=(P("section", "dp", None), P("section", "dp")),
        check_vma=False,
    )
```

profile of v0, /device:TPU:1, one launch (start us, length us, event | category | flops | bytes accessed | tf_op | source)
XLA Modules:
  0.0 1096.6 jit_solution(13001419332068599197)
XLA Ops:
  51.2 36.3 %all-reduce.5 = (bf16[1024]{0:T(1024)(128)(2,1)S(1)}, bf16[1024]{0:T(1024)(128)(2,1)S(1)}) all-reduce(bf16[1024]{0:T(1024)(128)(2,1)S(1)} %dynamic-update-slice.1, bf16[1024]{0:T(1024)(128)(2,1)S(1)} %dynamic-update-slice), channel_id=1, replica_groups=mesh['section'=16,'dp'=16] {'dp'}, use_global_device_ids=true, to_apply=%add.1 | all-reduce | flops 2048 | bytes 8192 | tf_op jit(solution)/shard_map/squeeze | solution.py:161
  88.4 207.6 %while.70 = (s32[]{:T(128)}, bf16[64,1024]{1,0:T(8,128)(2,1)S(1)}, bf16[2,64,1024]{2,1,0:T(8,128)(2,1)}, bf16[2,64,1024]{2,1,0:T(8,128)(2,1)S(1)}, f32[2,64,1024...) while((s32[]{:T(128)}, bf16[64,1024]{1,0:T(8,128)(2,1)S(1)}, ...), condition=%wide.region_16.17_spmd, body=%wide.region_12.16_spmd.sunk | while | flops 135726272 | bytes 4605351 | solution.py:241
  91.1 7.9 collective-permute-done.2
  101.8 6.5 collective-permute-done.2
  128.6 6.8 collective-permute-done.2
  138.1 6.8 collective-permute-done.2
  147.6 6.8 collective-permute-done.2
  157.1 6.8 collective-permute-done.2
  166.7 7.4 collective-permute-done.2
  176.8 8.5 collective-permute-done.2
  188.0 7.0 collective-permute-done.2
  197.7 6.3 collective-permute-done.2
  206.7 6.8 collective-permute-done.2
  216.2 6.8 collective-permute-done.2
  225.8 42.7 %collective-permute-done.2 = bf16[64,1024]{1,0:T(8,128)(2,1)S(1)} collective-permute-done((bf16[64,1024]{1,0:T(8,128)(2,1)S(1)}, bf16[64,1024]{1,0:T(8,128)(2,1)S(1)}, u32[]{:S(2)}, u32[]{:S(2)}) %collective-permute-start.2) | collective-permute-done | bytes 131104 | tf_op jit(solution)/shard_map/while/body/eval_jaxpr/ppermute | solution.py:16
  275.3 8.0 collective-permute-done.2
  298.6 192.1 %while.71 = (s32[]{:T(128)}, bf16[64,1024]{1,0:T(8,128)(2,1)S(1)}, f32[1024,1024]{1,0:T(8,128)}, f32[1024]{0:T(1024)S(1)}, s32[17]{0:T(128)S(1)}, /*index=5*/s32...) while((s32[]{:T(128)}, bf16[64,1024]{1,0:T(8,128)(2,1)S(1)}, ...), condition=%wide.region_22.23_spmd, body=%wide.region_17.22_spmd.sunk | while | flops 273482752 | bytes 46959320 | solution.py:243
  299.8 6.7 conditional.11
  312.4 6.7 conditional.11
  327.6 12.2 %collective-permute-start.3 = (bf16[64,1024]{1,0:T(8,128)(2,1)S(1)}, bf16[64,1024]{1,0:T(8,128)(2,1)S(1)}, u32[]{:S(2)}, u32[]{:S(2)}) collective-permute-start(bf16[64,1024]{1,0:T(8,128)(2,1)S(1)} %get-tuple-element.1363), channel_id=1, source_target_pairs={{0,16},{16,32},{32,48},{48,64},{64,80},{80,96},{96,112},{112,128},... | collective-permute-start | bytes 393224 | tf_op jit(solution)/shard_map/while/body/eval_jaxpr/ppermute | solution.py:16
  351.6 10.1 collective-permute-start.3
  364.9 6.2 collective-permute-start.3
  374.3 8.5 collective-permute-start.3
  396.3 8.8 collective-permute-start.3
  408.3 6.5 collective-permute-start.3
  418.0 6.7 collective-permute-start.3
  428.0 6.2 collective-permute-start.3
  437.4 7.6 collective-permute-start.3
  448.2 6.2 collective-permute-start.3
  457.6 7.5 collective-permute-start.3
  468.3 6.2 collective-permute-start.3
  477.7 11.0 %collective-permute-start.3 = (bf16[64,1024]{1,0:T(8,128)(2,1)S(1)}, bf16[64,1024]{1,0:T(8,128)(2,1)S(1)}, u32[]{:S(2)}, u32[]{:S(2)}) collective-permute-start(bf16[64,1024]{1,0:T(8,128)(2,1)S(1)} %get-tuple-element.1363), channel_id=1, source_target_pairs={{0,16},{16,32},{32,48},{48,64},{64,80},{80,96},{96,112},{112,128},... | collective-permute-start | bytes 393224 | tf_op jit(solution)/shard_map/while/body/eval_jaxpr/ppermute | solution.py:16
  495.8 187.2 %while.68 = (s32[]{:T(128)}, bf16[64,1024]{1,0:T(8,128)(2,1)S(1)}, bf16[2,64,1024]{2,1,0:T(8,128)(2,1)}, bf16[2,64,1024]{2,1,0:T(8,128)(2,1)S(1)}, f32[2,64,1024...) while((s32[]{:T(128)}, bf16[64,1024]{1,0:T(8,128)(2,1)S(1)}, ...), condition=%wide.region_4.5_spmd, body=%wide.region_0.4_spmd.sunk | while | flops 135726272 | bytes 4605351 | solution.py:240
  521.5 8.5 collective-permute-start
  542.3 9.4 collective-permute-start
  564.3 7.5 collective-permute-start
  574.9 8.2 collective-permute-start
  586.2 8.3 collective-permute-start
  597.9 9.1 collective-permute-start
  620.3 9.8 collective-permute-start
  642.9 6.6 collective-permute-start
  653.4 7.7 collective-permute-start
  664.3 6.4 collective-permute-start
  673.8 7.2 collective-permute-start
  685.5 271.4 %while.69 = (s32[]{:T(128)}, bf16[64,1024]{1,0:T(8,128)(2,1)S(1)}, f32[1024,1024]{1,0:T(8,128)}, f32[1024]{0:T(1024)S(1)}, s32[17]{0:T(128)S(1)}, /*index=5*/s32...) while((s32[]{:T(128)}, bf16[64,1024]{1,0:T(8,128)(2,1)S(1)}, ...), condition=%wide.region_10.11_spmd, body=%wide.region_5.10_spmd.sunk | while | flops 273482752 | bytes 46959320 | solution.py:242
  688.1 9.3 collective-permute-done.1
  700.0 8.3 collective-permute-done.1
  711.0 8.7 collective-permute-done.1
  722.3 8.0 collective-permute-done.1
  732.9 6.8 collective-permute-done.1
  742.3 8.3 collective-permute-done.1
  753.3 8.4 collective-permute-done.1
  764.4 8.4 collective-permute-done.1
  775.4 10.1 collective-permute-done.1
  788.2 9.3 collective-permute-done.1
  800.1 7.8 collective-permute-done.1
  810.6 7.7 collective-permute-done.1
  821.0 7.4 collective-permute-done.1
  831.0 7.7 collective-permute-done.1
  841.4 83.0 %collective-permute-done.1 = bf16[64,1024]{1,0:T(8,128)(2,1)S(1)} collective-permute-done((bf16[64,1024]{1,0:T(8,128)(2,1)S(1)}, bf16[64,1024]{1,0:T(8,128)(2,1)S(1)}, u32[]{:S(2)}, u32[]{:S(2)}) %collective-permute-start.1) | collective-permute-done | bytes 131104 | tf_op jit(solution)/shard_map/while/body/eval_jaxpr/ppermute | solution.py:16
  925.6 6.7 conditional.9
  933.6 8.0 collective-permute-done.1
  943.0 6.7 conditional.9
  970.8 98.9 %all-reduce.4 = (bf16[1024]{0:T(1024)(128)(2,1)S(1)}, bf16[1024]{0:T(1024)(128)(2,1)S(1)}) all-reduce(bf16[1024]{0:T(1024)(128)(2,1)S(1)} %convert_element_type.158, bf16[1024]{0:T(1024)(128)(2,1)S(1)} %convert_element_type.160), channel_id=4, replica_groups=mesh['section'=16,'dp'=16] {'dp'}, use_global_device_ids=true, to_apply=%region_24.25.clone | all-reduce | flops 2048 | bytes 8192
  (438 shorter events, 381.3 us)
Async XLA Ops:
  7.2 80.4 %all-gather.5.cloned.1.call-start = ((), (), s32[]{:S(2)}) async-start(), calls=%async_computation.4 | async-start | bytes 2228224 | tf_op jit(solution)/shard_map/all_gather | solution.py:154
  24.9 8.5 collective-permute-start.11
  34.1 460.8 %all-gather.3.cloned.1.call-start = ((), (), s32[]{:S(2)}) async-start(), calls=%async_computation.2 | async-start | bytes 2228224 | tf_op jit(solution)/shard_map/all_gather | solution.py:152
  34.9 926.0 %reduce-scatter.5.cloned.1.call-start = ((), (), s32[]{:S(2)}) async-start(), calls=%async_computation.5 | async-start | bytes 2228224 | tf_op jit(solution)/shard_map/reduce_scatter | solution.py:251
  89.8 9.2 collective-permute-start.2
  100.5 7.8 collective-permute-start.2
  127.3 8.1 collective-permute-start.2
  136.8 8.1 collective-permute-start.2
  146.3 8.1 collective-permute-start.2
  155.8 8.1 collective-permute-start.2
  165.4 8.7 collective-permute-start.2
  175.5 9.8 collective-permute-start.2
  186.7 8.3 collective-permute-start.2
  205.4 8.1 collective-permute-start.2
  214.9 8.1 collective-permute-start.2
  224.5 44.0 %collective-permute-start.2 = (bf16[64,1024]{1,0:T(8,128)(2,1)S(1)}, bf16[64,1024]{1,0:T(8,128)(2,1)S(1)}, u32[]{:S(2)}, u32[]{:S(2)}) collective-permute-start(bf16[64,1024]{1,0:T(8,128)(2,1)S(1)} %get-tuple-element.1344), channel_id=1, source_target_pairs={{16,0},{32,16},{48,32},{64,48},{80,64},{96,80},{112,96},{128,112},... | collective-permute-start | bytes 393224 | tf_op jit(solution)/shard_map/while/body/eval_jaxpr/ppermute | solution.py:16
  274.0 9.3 collective-permute-start.2
  327.6 14.2 %collective-permute-start.3 = (bf16[64,1024]{1,0:T(8,128)(2,1)S(1)}, bf16[64,1024]{1,0:T(8,128)(2,1)S(1)}, u32[]{:S(2)}, u32[]{:S(2)}) collective-permute-start(bf16[64,1024]{1,0:T(8,128)(2,1)S(1)} %get-tuple-element.1363), channel_id=1, source_target_pairs={{0,16},{16,32},{32,48},{48,64},{64,80},{80,96},{96,112},{112,128},... | collective-permute-start | bytes 393224 | tf_op jit(solution)/shard_map/while/body/eval_jaxpr/ppermute | solution.py:16
  351.6 12.0 %collective-permute-start.3 = (bf16[64,1024]{1,0:T(8,128)(2,1)S(1)}, bf16[64,1024]{1,0:T(8,128)(2,1)S(1)}, u32[]{:S(2)}, u32[]{:S(2)}) collective-permute-start(bf16[64,1024]{1,0:T(8,128)(2,1)S(1)} %get-tuple-element.1363), channel_id=1, source_target_pairs={{0,16},{16,32},{32,48},{48,64},{64,80},{80,96},{96,112},{112,128},... | collective-permute-start | bytes 393224 | tf_op jit(solution)/shard_map/while/body/eval_jaxpr/ppermute | solution.py:16
  364.9 8.1 collective-permute-start.3
  374.3 11.5 %collective-permute-start.3 = (bf16[64,1024]{1,0:T(8,128)(2,1)S(1)}, bf16[64,1024]{1,0:T(8,128)(2,1)S(1)}, u32[]{:S(2)}, u32[]{:S(2)}) collective-permute-start(bf16[64,1024]{1,0:T(8,128)(2,1)S(1)} %get-tuple-element.1363), channel_id=1, source_target_pairs={{0,16},{16,32},{32,48},{48,64},{64,80},{80,96},{96,112},{112,128},... | collective-permute-start | bytes 393224 | tf_op jit(solution)/shard_map/while/body/eval_jaxpr/ppermute | solution.py:16
  387.1 7.8 collective-permute-start.3
  396.3 10.7 collective-permute-start.3
  408.3 8.4 collective-permute-start.3
  418.0 8.6 collective-permute-start.3
  428.0 8.1 collective-permute-start.3
  437.4 9.5 collective-permute-start.3
  448.2 8.1 collective-permute-start.3
  457.6 9.4 collective-permute-start.3
  468.3 8.1 collective-permute-start.3
  477.7 12.9 %collective-permute-start.3 = (bf16[64,1024]{1,0:T(8,128)(2,1)S(1)}, bf16[64,1024]{1,0:T(8,128)(2,1)S(1)}, u32[]{:S(2)}, u32[]{:S(2)}) collective-permute-start(bf16[64,1024]{1,0:T(8,128)(2,1)S(1)} %get-tuple-element.1363), channel_id=1, source_target_pairs={{0,16},{16,32},{32,48},{48,64},{64,80},{80,96},{96,112},{112,128},... | collective-permute-start | bytes 393224 | tf_op jit(solution)/shard_map/while/body/eval_jaxpr/ppermute | solution.py:16
  494.6 593.8 %reduce-scatter.3.cloned.1.call-start = ((), (), s32[]{:S(2)}) async-start(), calls=%async_computation.3 | async-start | bytes 2228224 | tf_op jit(solution)/shard_map/reduce_scatter | solution.py:245
  500.2 8.0 collective-permute-start
  521.5 10.4 collective-permute-start
  533.1 8.0 collective-permute-start
  542.3 12.4 %collective-permute-start = (bf16[64,1024]{1,0:T(8,128)(2,1)S(1)}, bf16[64,1024]{1,0:T(8,128)(2,1)S(1)}, u32[]{:S(2)}, u32[]{:S(2)}) collective-permute-start(bf16[64,1024]{1,0:T(8,128)(2,1)S(1)} %get-tuple-element.1310), channel_id=1, source_target_pairs={{0,16},{16,32},{32,48},{48,64},{64,80},{80,96},{96,112},{112,128},... | collective-permute-start | bytes 393224 | tf_op jit(solution)/shard_map/while/body/eval_jaxpr/ppermute | solution.py:16
  564.3 9.4 collective-permute-start
  574.9 10.1 collective-permute-start
  586.2 10.4 collective-permute-start
  597.9 12.4 %collective-permute-start = (bf16[64,1024]{1,0:T(8,128)(2,1)S(1)}, bf16[64,1024]{1,0:T(8,128)(2,1)S(1)}, u32[]{:S(2)}, u32[]{:S(2)}) collective-permute-start(bf16[64,1024]{1,0:T(8,128)(2,1)S(1)} %get-tuple-element.1310), channel_id=1, source_target_pairs={{0,16},{16,32},{32,48},{48,64},{64,80},{80,96},{96,112},{112,128},... | collective-permute-start | bytes 393224 | tf_op jit(solution)/shard_map/while/body/eval_jaxpr/ppermute | solution.py:16
  620.3 12.2 %collective-permute-start = (bf16[64,1024]{1,0:T(8,128)(2,1)S(1)}, bf16[64,1024]{1,0:T(8,128)(2,1)S(1)}, u32[]{:S(2)}, u32[]{:S(2)}) collective-permute-start(bf16[64,1024]{1,0:T(8,128)(2,1)S(1)} %get-tuple-element.1310), channel_id=1, source_target_pairs={{0,16},{16,32},{32,48},{48,64},{64,80},{80,96},{96,112},{112,128},... | collective-permute-start | bytes 393224 | tf_op jit(solution)/shard_map/while/body/eval_jaxpr/ppermute | solution.py:16
  633.7 7.9 collective-permute-start
  642.9 9.4 collective-permute-start
  653.4 9.7 collective-permute-start
  664.3 8.3 collective-permute-start
  673.8 9.1 collective-permute-start
  686.8 10.6 collective-permute-start.1
  698.7 9.6 collective-permute-start.1
  709.7 10.0 collective-permute-start.1
  721.0 9.3 collective-permute-start.1
  731.6 8.1 collective-permute-start.1
  741.0 9.6 collective-permute-start.1
  752.0 9.7 collective-permute-start.1
  763.0 9.7 collective-permute-start.1
  774.1 11.4 %collective-permute-start.1 = (bf16[64,1024]{1,0:T(8,128)(2,1)S(1)}, bf16[64,1024]{1,0:T(8,128)(2,1)S(1)}, u32[]{:S(2)}, u32[]{:S(2)}) collective-permute-start(bf16[64,1024]{1,0:T(8,128)(2,1)S(1)} %get-tuple-element.1329), channel_id=1, source_target_pairs={{16,0},{32,16},{48,32},{64,48},{80,64},{96,80},{112,96},{128,112},... | collective-permute-start | bytes 393224 | tf_op jit(solution)/shard_map/while/body/eval_jaxpr/ppermute | solution.py:16
  786.9 10.6 collective-permute-start.1
  798.8 9.2 collective-permute-start.1
  809.3 9.0 collective-permute-start.1
  819.7 8.7 collective-permute-start.1
  829.7 9.0 collective-permute-start.1
  840.1 84.3 %collective-permute-start.1 = (bf16[64,1024]{1,0:T(8,128)(2,1)S(1)}, bf16[64,1024]{1,0:T(8,128)(2,1)S(1)}, u32[]{:S(2)}, u32[]{:S(2)}) collective-permute-start(bf16[64,1024]{1,0:T(8,128)(2,1)S(1)} %get-tuple-element.1329), channel_id=1, source_target_pairs={{16,0},{32,16},{48,32},{64,48},{80,64},{96,80},{112,96},{128,112},... | collective-permute-start | bytes 393224 | tf_op jit(solution)/shard_map/while/body/eval_jaxpr/ppermute | solution.py:16
  932.3 9.3 collective-permute-start.1
  970.3 110.0 %collective-permute-start.14 = (bf16[64,1024]{1,0:T(8,128)(2,1)S(1)}, bf16[64,1024]{1,0:T(8,128)(2,1)S(1)}, u32[]{:S(2)}, u32[]{:S(2)}) collective-permute-start(bf16[64,1024]{1,0:T(8,128)(2,1)S(1)} %collective-permute-done.13), channel_id=1, source_target_pairs={{0,64},{16,80},{32,96},{48,112},{64,0},{80,16},{96,32},{112,48},{1... | collective-permute-start | bytes 393224 | tf_op jit(solution)/shard_map/ppermute | solution.py:20
  1080.2 8.2 collective-permute-start.15
  (38 other events, 174.5 us)
Sparse Core Ops, SparseCore 0:
  34.2 42.6 all-gather.4
  78.8 41.0 all-gather.2
  494.8 144.0 reduce-scatter.4
  960.9 127.4 reduce-scatter.2
where the time goes:
time: 1100 us
  waiting for transfers between devices  473 us (43%)
  starting transfers between devices  321 us (29%)
  blocking collectives  135 us (12%)
  local copies, waits for them, and re-layouts  60.8 us (6%)
  loops' own time  47.5 us (4%)
  matrix products  23 us (2%)
  other arithmetic  20 us (2%)
  between operations  15.1 us (1%)
    ppermute x68, waiting for transfers between devices, passed_along(): return lax.ppermute(block, axis, route)  439 us
    ppermute x68, starting transfers between devices, passed_along(): return lax.ppermute(block, axis, route)  288 us
    unnamed x1, blocking collectives  98.9 us
    dynamic_slice x68, local copies, waits for them, and re-layouts, shards(): lax.scan(down_forward_step, (empty_rows, empty_saved), counters)  42.3 us
    squeeze x1, blocking collectives, shards(): far_gain[0]  36.3 us
    ppermute x16, starting transfers between devices, from_partner(): lax.ppermute(x, axis, [(i, i ^ 1 << stride) for i in range(lax.axis_size(...  33.3 us
    ppermute x16, waiting for transfers between devices, from_partner(): lax.ppermute(x, axis, [(i, i ^ 1 << stride) for i in range(lax.axis_size(...  32.2 us
  transfers between devices with their start and end apart: 88, of which 83 were waited for; matrix products, arithmetic and copies ran while one was open for 9% of the time, Pallas kernels for 0%

commit v1 on v0

v1 whole, which is shorter than its diff:
```python
import functools
import math

import jax
import jax.numpy as jnp
from jax import lax
from jax.experimental import pallas as pl
from jax.experimental.pallas import tpu as pltpu
from jax.sharding import PartitionSpec as P

EPSILON = 1e-05
CUBIC = 0.044715
SLOPE = math.sqrt(2.0 / math.pi)
MESH = pl.DeviceIdType.MESH
FIRST_PAIR = 8
D = 1024
HALF = D // 2
MB_ROWS = 32


def kernel(
    down_in, up_in, down_cot, up_cot, w_in, g_in, gw_out, gg_out,
    w, part, r0, r1a, r1b, s1a, s1b, r2a, r2b, zres, zsend, h, du, xs, sl, rinv, xo, do, cot,
    zx_s, zx_r, a1_s, a1_r, b1_s, b1_r, a2_s, a2_r, b2_s, b2_r, d_s, d_r,
    fx_s, fx_r, bx_s, bx_r, r0_s, r0_r, r1a_s, r1a_r, r1b_s, r1b_r, r2a_s, r2a_r, r2b_s, r2b_r,
    zr_s, zr_r,
):
    sec, dp = lax.axis_index("section"), lax.axis_index("dp")
    z, xh = sec // 2, sec % 2
    y, xl, c = dp // 4, (dp // 2) % 2, dp % 2
    x = xh * 2 + xl
    other = 1 - c

    def at(ax, ay, az, ac):
        return (az * 2 + ax // 2, ay * 4 + (ax % 2) * 2 + ac)

    def xdev(k):
        return at((x + k) % 4, y, z, c)

    def ydev(k):
        return at(x, (y + k) % 4, z, c)

    def zdev(k):
        return at(x, y, (z + 8 + k) % 8, c)

    sibling = at(x, y, z, other)
    pair = z >= FIRST_PAIR
    single = z < FIRST_PAIR
    ispair = pair.astype(jnp.int32) if FIRST_PAIR < 8 else 0
    odd = (z % 2) * ispair
    planes = 1 + ispair
    layers = 2 * planes
    slots = 4 // planes
    own_p = odd
    own_l = 2 * own_p + xh
    zpartner = at(x, y, z + 1 - 2 * (z % 2), c)

    barrier = pltpu.get_barrier_semaphore()
    peers = [sibling] + [xdev(k) for k in (1, 2, 3)] + [ydev(k) for k in (1, 2, 3)]
    peers += [zdev(1), zdev(-1)]
    if FIRST_PAIR < 8:
        peers += [zdev(2), zdev(-2)]
    for peer in peers:
        pl.semaphore_signal(barrier, inc=1, device_id=peer, device_id_type=MESH)

    def send(src, dst, ss, rs, to):
        return pltpu.make_async_remote_copy(
            src_ref=src, dst_ref=dst, send_sem=ss, recv_sem=rs, device_id=to, device_id_type=MESH
        )

    eye = lax.broadcasted_iota(jnp.int32, (64, 64), 0) == lax.broadcasted_iota(jnp.int32, (64, 64), 1)
    gain_col = jnp.sum(jnp.where(eye, g_in[...].astype(jnp.float32), 0.0), axis=1, keepdims=True)
    w[own_l, y, xl, c] = (w_in[0].astype(jnp.float32) * gain_col).astype(jnp.bfloat16)
    pl.semaphore_wait(barrier, len(peers))

    A, B, ALL = pl.ds(0, HALF), pl.ds(HALF, HALF), pl.ds(0, D)

    def blk(p, bx, by, cols):
        return w.at[2 * p + bx // 2, by, bx % 2, c, :, cols]

    def row_of(p, by):
        return w.at[pl.ds(2 * p, 2), by, :, c, :, A]

    def col_of(p, bx):
        return w.at[2 * p + bx // 2, :, bx % 2, c, :, B]

    def zx():
        ref = w.at[own_l, y, xl, c]
        return send(ref, ref, zx_s, zx_r, zpartner)

    def zx_other():
        ref = w.at[2 * (1 - own_p) + xh, y, xl, c]
        return send(ref, ref, zx_s, zx_r, zpartner)

    def a1(p, k):
        ref = blk(p, x, y, A)
        return send(ref, ref, a1_s.at[p, k - 1], a1_r.at[p, k - 1], xdev(k))

    def b1(p, k):
        ref = blk(p, x, y, B)
        return send(ref, ref, b1_s.at[p, k - 1], b1_r.at[p, k - 1], ydev(k))

    def a2(p, src, k):
        ref = blk(p, (x - src + 4) % 4, y, A)
        return send(ref, ref, a2_s.at[p, src, k - 1], a2_r.at[p, k - 1], ydev(k))

    def b2(p, src, k):
        ref = blk(p, x, (y - src + 4) % 4, B)
        return send(ref, ref, b2_s.at[p, src, k - 1], b2_r.at[p, k - 1], xdev(k))

    def a2_wait(p, k):
        ref = row_of(p, (y - k + 4) % 4)
        return send(ref, ref, a2_s.at[p, 0, 0], a2_r.at[p, k - 1], sibling)

    def b2_wait(p, k):
        ref = col_of(p, (x - k + 4) % 4)
        return send(ref, ref, b2_s.at[p, 0, 0], b2_r.at[p, k - 1], sibling)

    def d_own(p):
        ref = blk(p, x, y, ALL)
        return send(ref, ref, d_s.at[p, 0], d_r.at[p], sibling)

    def d_a1(p, k):
        ref = blk(p, (x - k + 4) % 4, y, A)
        return send(ref, ref, d_s.at[p, k], d_r.at[p], sibling)

    def d_b1(p, k):
        ref = blk(p, x, (y - k + 4) % 4, B)
        return send(ref, ref, d_s.at[p, 3 + k], d_r.at[p], sibling)

    def d_a2(p, k):
        ref = row_of(p, (y - k + 4) % 4)
        return send(ref, ref, d_s.at[p, 6 + k], d_r.at[p], sibling)

    def d_b2(p, k):
        ref = col_of(p, (x - k + 4) % 4)
        return send(ref, ref, d_s.at[p, 9 + k], d_r.at[p], sibling)

    def d_wait(p):
        ref = w.at[pl.ds(2 * p, 2), :, :, other]
        return send(ref, ref, d_s.at[p, 0], d_r.at[p], sibling)

    K = (1, 2, 3)
    if FIRST_PAIR < 8:

        @pl.when(pair)
        def _():
            zx().start()

    def gather_start(i, carry):
        p = (own_p + i) % planes

        @pl.when(i > 0)
        def _():
            zx_other().wait_recv()

        for k in K:
            a1(p, k).start()
            b1(p, k).start()
        for k in K:
            a2(p, 0, k).start()
            b2(p, 0, k).start()
        d_own(p).start()
        return carry

    def gather_mid(i, carry):
        p = (own_p + i) % planes
        for src in (1, 3, 2):
            a1(p, src).wait_recv()
            for k in K:
                a2(p, src, k).start()
            d_a1(p, src).start()
            b1(p, src).wait_recv()
            for k in K:
                b2(p, src, k).start()
            d_b1(p, src).start()
        return carry

    def gather_end(i, carry):
        p = (own_p + i) % planes
        for k in (1, 3, 2):
            a2_wait(p, k).wait_recv()
            d_a2(p, k).start()
            b2_wait(p, k).wait_recv()
            d_b2(p, k).start()
        return carry

    def gather_wait(i, carry):
        d_wait((own_p + i) % planes).wait_recv()
        return carry

    lax.fori_loop(0, planes, gather_start, 0)

    first = z < (2 if FIRST_PAIR == 0 else 1)
    last = z >= (7 if FIRST_PAIR == 8 else 6)

    def load_rows(dst, down, up):
        for slot in range(4):
            def take(j, slot=slot):
                b, half = j // 2, j % 2
                for ref, cond in ((down, xh == 0), (up, xh == 1)):

                    @pl.when(cond)
                    def _(ref=ref):
                        dst[slot] = ref[b, pl.ds(pl.multiple_of(half * MB_ROWS, MB_ROWS), MB_ROWS), :]

            if FIRST_PAIR == 8:
                take(slot)
            elif slot < 2:
                take((2 * slot + odd) if FIRST_PAIR == 0 else slot * planes + odd)
            else:

                @pl.when(single)
                def _(slot=slot):
                    take(slot)

    @pl.when(first)
    def _():
        load_rows(xs.at[0], down_in, up_in)

    @pl.when(last)
    def _():
        load_rows(cot, down_cot, up_cot)

    if FIRST_PAIR < 8:
        h[...] = jnp.zeros_like(h)
        du[...] = jnp.zeros_like(du)

    lax.fori_loop(0, planes, gather_mid, 0)
    lax.fori_loop(0, planes, gather_end, 0)
    lax.fori_loop(0, planes, gather_wait, 0)

    if FIRST_PAIR == 8:

        def f_route(j):
            return zdev(1), j

        def b_route(j):
            return zdev(-1), j

    else:
        to_pair = (z == FIRST_PAIR - 1).astype(jnp.int32)
        from_pair = ((z // 2) * 2 == FIRST_PAIR).astype(jnp.int32)

        def f_route(j):
            step = ispair * 2 + (1 - ispair) * (1 + to_pair * (j % 2))
            slot = j - to_pair * (j - j // 2)
            return zdev(step), slot

        def b_route(j):
            step = ispair * (2 + from_pair * (odd - 1)) + (1 - ispair)
            slot = j + from_pair * (j + odd)
            return zdev(-step), slot

    def fx(j):
        to, slot = f_route(j)
        return send(xo.at[j], xs.at[0, slot], fx_s.at[j], fx_r.at[slot], to)

    def fx_wait(j):
        return send(xo.at[j], xs.at[0, j], fx_s.at[j], fx_r.at[j], sibling)

    def bx(j):
        to, slot = b_route(j)
        return send(do.at[j], cot.at[slot], bx_s.at[j], bx_r.at[slot], to)

    def bx_wait(j):
        return send(do.at[j], cot.at[j], bx_s.at[j], bx_r.at[j], sibling)

    def forward(j, carry):
        @pl.when(jnp.logical_not(first))
        def _():
            fx_wait(j).wait_recv()

        rows = pl.ds(pl.multiple_of(j * MB_ROWS, MB_ROWS), MB_ROWS)

        def layer(l, carry):
            xf = xs[l, j].astype(jnp.float32)
            r = lax.rsqrt(jnp.mean(xf * xf, axis=-1, keepdims=True) + EPSILON)
            normed = (xf * r).astype(jnp.bfloat16)
            h[l, rows, :] = normed
            rinv[l, j] = jnp.broadcast_to(r, (MB_ROWS, 128))
            u = jnp.dot(normed, w[l].reshape(D, D), preferred_element_type=jnp.float32)
            u2 = u * u
            t = jnp.tanh(SLOPE * (u + CUBIC * u2 * u))
            nxt = (xf + 0.5 * u * (1.0 + t)).astype(jnp.bfloat16)

            @pl.when(l < layers - 1)
            def _():
                xs[l + 1, j] = nxt

            @pl.when(l == layers - 1)
            def _():
                xo[j] = nxt

                @pl.when(jnp.logical_not(last))
                def _():
                    fx(j).start()

            sl[l, j] = 0.5 * (1.0 + t) + 0.5 * u * (1.0 - t * t) * SLOPE * (1.0 + 3.0 * CUBIC * u2)
            return carry

        return lax.fori_loop(0, layers, layer, carry)

    lax.fori_loop(0, slots, forward, 0)

    def backward(j, carry):
        @pl.when(jnp.logical_not(last))
        def _():
            bx_wait(j).wait_recv()

        rows = pl.ds(pl.multiple_of(j * MB_ROWS, MB_ROWS), MB_ROWS)

        def layer(i, carry):
            l = layers - 1 - i
            df = cot[j].astype(jnp.float32)
            grad = (df * sl[l, j]).astype(jnp.bfloat16)
            du[l, rows, :] = grad

            @pl.when(jnp.logical_not(jnp.logical_and(first, l == 0)))
            def _():
                a = lax.dot_general(
                    grad, w[l].reshape(D, D), (((1,), (1,)), ((), ())), preferred_element_type=jnp.float32
                )
                r = rinv[l, j][:, 0:1]
                xr = xs[l, j].astype(jnp.float32) * r
                new = (df + r * (a - xr * jnp.mean(a * xr, axis=-1, keepdims=True))).astype(jnp.bfloat16)

                @pl.when(l > 0)
                def _():
                    cot[j] = new

                @pl.when(l == 0)
                def _():
                    do[j] = new
                    bx(j).start()

            return carry

        return lax.fori_loop(0, layers, layer, carry)

    lax.fori_loop(0, slots, backward, 0)

    def e0(l):
        return send(part.at[l, :, :, other], r0.at[l], r0_s.at[l], r0_r.at[l], sibling)

    def e1a(l, k):
        return send(
            r0.at[l, (y + k) % 4, :, :, A], r1a.at[l, k - 1], r1a_s.at[l, k - 1], r1a_r.at[l, k - 1], ydev(k)
        )

    def e1b(l, k):
        return send(
            r0.at[l, :, (x + k) % 2, :, B], r1b.at[l // 2, k - 1], r1b_s.at[l, k - 1], r1b_r.at[l // 2, k - 1], xdev(k)
        )

    def e2a(l, k):
        return send(
            s1a.at[l, (x + k) % 2], r2a.at[l // 2, k - 1], r2a_s.at[l, k - 1], r2a_r.at[l // 2, k - 1], xdev(k)
        )

    def e2b(l, k):
        p = l // 2
        return send(
            s1b.at[p, (y + k) % 4], r2b.at[p, k - 1], r2b_s.at[p, k - 1], r2b_r.at[p, k - 1], ydev(k)
        )

    def for_x(l, act):
        for k in K:

            @pl.when(((x + k) % 4) // 2 == l % 2)
            def _(k=k):
                act(k)

    def mine(l):
        return xh == l % 2

    def f32(v):
        return v.astype(jnp.float32)

    def reduce_a(i, carry):
        l = layers - 1 - i
        g = lax.dot_general(
            h[l], du[l], (((0,), (0,)), ((), ())), preferred_element_type=jnp.float32
        )
        part[l] = g.astype(jnp.bfloat16).reshape(4, 2, 2, 64, D)
        e0(l).start()
        return carry

    def reduce_b(i, carry):
        l = layers - 1 - i
        e0(l).wait_recv()
        r0[l] = (f32(r0[l]) + f32(part[l, :, :, c])).astype(jnp.bfloat16)
        for k in K:
            e1a(l, k).start()
        for_x(l, lambda k: e1b(l, k).start())
        return carry

    def reduce_c(i, carry):
        l = layers - 1 - i
        for k in K:
            e1a(l, k).wait_recv()
        s1a[l] = (f32(r0[l, y, :, :, 0:HALF]) + f32(r1a[l, 0]) + f32(r1a[l, 1]) + f32(r1a[l, 2])).astype(jnp.bfloat16)
        for_x(l, lambda k: e2a(l, k).start())

        @pl.when(mine(l))
        def _():
            p = l // 2
            for k in K:
                e1b(l, k).wait_recv()
            s1b[p] = (f32(r0[l, :, xl, :, HALF:D]) + f32(r1b[p, 0]) + f32(r1b[p, 1]) + f32(r1b[p, 2])).astype(jnp.bfloat16)
            for k in K:
                e2b(l, k).start()

        return carry

    def zr():
        return send(zsend, zres, zr_s, zr_r, zpartner)

    def total(l):
        p = l // 2
        for k in K:
            e2a(l, k).wait_recv()
            e2b(l, k).wait_recv()
        left = f32(s1a[l, xl]) + f32(r2a[p, 0]) + f32(r2a[p, 1]) + f32(r2a[p, 2])
        right = f32(s1b[p, y]) + f32(r2b[p, 0]) + f32(r2b[p, 1]) + f32(r2b[p, 2])
        return left, right

    lax.fori_loop(0, layers, reduce_a, 0)
    lax.fori_loop(0, layers, reduce_b, 0)
    lax.fori_loop(0, layers, reduce_c, 0)

    if FIRST_PAIR < 8:

        @pl.when(pair)
        def _():
            left, right = total(2 * (1 - own_p) + xh)
            zsend[:, 0:HALF] = left
            zsend[:, HALF:D] = right
            zr().start()

    left, right = total(own_l)
    gw_out[0, :, 0:HALF] = left
    gw_out[0, :, HALF:D] = right
    if FIRST_PAIR < 8:

        @pl.when(pair)
        def _():
            zr().wait_recv()
            gw_out[0] = gw_out[0] + zres[...]

    full = gw_out[0]
    per_row = jnp.sum(full * w_in[0].astype(jnp.float32), axis=1, keepdims=True)
    gg_out[...] = jnp.sum(jnp.where(eye, per_row, 0.0), axis=0, keepdims=True)
    gw_out[0] = full * gain_col

    if FIRST_PAIR < 8:

        @pl.when(pair)
        def _():
            zx().wait_send()
            zr().wait_send()

    def drain_gather(i, carry):
        p = (own_p + i) % planes
        for k in K:
            a1(p, k).wait_send()
            b1(p, k).wait_send()
            for src in range(4):
                a2(p, src, k).wait_send()
                b2(p, src, k).wait_send()
            d_a1(p, k).wait_send()
            d_b1(p, k).wait_send()
            d_a2(p, k).wait_send()
            d_b2(p, k).wait_send()
        d_own(p).wait_send()
        return carry

    lax.fori_loop(0, planes, drain_gather, 0)

    def drain_relay(j, carry):
        @pl.when(jnp.logical_not(last))
        def _():
            fx(j).wait_send()

        @pl.when(jnp.logical_not(first))
        def _():
            bx(j).wait_send()

        return carry

    lax.fori_loop(0, slots, drain_relay, 0)

    def drain_reduce(l, carry):
        e0(l).wait_send()
        for k in K:
            e1a(l, k).wait_send()
        for_x(l, lambda k: e1b(l, k).wait_send())
        for_x(l, lambda k: e2a(l, k).wait_send())

        @pl.when(mine(l))
        def _():
            for k in K:
                e2b(l, k).wait_send()

        return carry

    lax.fori_loop(0, layers, drain_reduce, 0)


def shards(down_input, up_input, down_cot, up_cot, weight, gain):
    nl = 2 if FIRST_PAIR == 8 else 4
    np_ = nl // 2
    bf, f4 = jnp.bfloat16, jnp.float32
    dma = pltpu.SemaphoreType.DMA
    scratch = [
        pltpu.VMEM((nl, 4, 2, 2, 64, D), bf),
        pltpu.VMEM((nl, 4, 2, 2, 64, D), bf),
        pltpu.VMEM((nl, 4, 2, 64, D), bf),
        pltpu.VMEM((nl, 3, 2, 64, HALF), bf),
        pltpu.VMEM((np_, 3, 4, 64, HALF), bf),
        pltpu.VMEM((nl, 2, 64, HALF), bf),
        pltpu.VMEM((np_, 4, 64, HALF), bf),
        pltpu.VMEM((np_, 3, 64, HALF), bf),
        pltpu.VMEM((np_, 3, 64, HALF), bf),
        pltpu.VMEM((64, D), f4),
        pltpu.VMEM((64, D), f4),
        pltpu.VMEM((nl, 4 * MB_ROWS, D), bf),
        pltpu.VMEM((nl, 4 * MB_ROWS, D), bf),
        pltpu.VMEM((nl, 4, MB_ROWS, D), bf),
        pltpu.VMEM((nl, 4, MB_ROWS, D), f4),
        pltpu.VMEM((nl, 4, MB_ROWS, 128), f4),
        pltpu.VMEM((4, MB_ROWS, D), bf),
        pltpu.VMEM((4, MB_ROWS, D), bf),
        pltpu.VMEM((4, MB_ROWS, D), bf),
        dma, dma,
        dma((np_, 3)), dma((np_, 3)), dma((np_, 3)), dma((np_, 3)),
        dma((np_, 4, 3)), dma((np_, 3)), dma((np_, 4, 3)), dma((np_, 3)),
        dma((np_, 13)), dma((np_,)),
        dma((4,)), dma((4,)), dma((4,)), dma((4,)),
        dma((nl,)), dma((nl,)),
        dma((nl, 3)), dma((nl, 3)), dma((nl, 3)), dma((np_, 3)),
        dma((nl, 3)), dma((np_, 3)), dma((np_, 3)), dma((np_, 3)),
        dma, dma,
    ]
    vmem = pl.BlockSpec(memory_space=pltpu.VMEM)
    return pl.pallas_call(
        kernel,
        out_shape=(
            jax.ShapeDtypeStruct((1, 64, D), f4),
            jax.ShapeDtypeStruct((1, 64), f4),
        ),
        in_specs=[vmem] * 6,
        out_specs=(vmem, vmem),
        scratch_shapes=scratch,
        compiler_params=pltpu.CompilerParams(
            collective_id=0, has_side_effects=True, vmem_limit_bytes=56 * 1024 * 1024
        ),
    )(down_input, up_input, down_cot, up_cot, weight, gain)


def solution(mesh):
    rows = P(None, "dp", None)
    return jax.shard_map(
        shards,
        mesh=mesh,
        in_specs=(rows, rows, rows, rows, P("section", "dp", None), P("section", "dp")),
        out_specs=(P("section", "dp", None), P("section", "dp")),
        check_vma=False,
    )
```

time: 1100 us -> 135 us (0.12)
  waiting for transfers between devices: 473 us -> 0 us
  starting transfers between devices: 321 us -> 0 us
  blocking collectives: 135 us -> 0 us
  Pallas kernels: 0 us -> 132 us
  local copies, waits for them, and re-layouts: 60.8 us -> 2.19 us
  loops' own time: 47.5 us -> 0 us
  matrix products: 23 us -> 0 us
  other arithmetic: 20 us -> 0 us
  between operations: 15.1 us -> 0.65 us
    ppermute x84 -> x0, waiting for transfers between devices: 471 us -> none  [the longest x68 439 us: passed_along(): return lax.ppermute(block, axis, route)]
    ppermute x84 -> x0, starting transfers between devices: 321 us -> none  [the longest x68 288 us: passed_along(): return lax.ppermute(block, axis, route)]
    pallas_call x0 -> x1, Pallas kernels: none -> 132 us  [shards(): pl.pallas_call(kernel, out_shape=(jax.ShapeDtypeStruct((1, 64, D), f4), j...]
    unnamed x1 -> x0, blocking collectives: 98.9 us -> none
    another operation x72 -> x0, loops' own time: 47.5 us -> none  [the longest x1 12.3 us: shards(): lax.scan(up_forward_step, (empty_rows, empty_saved), counters)]
    dynamic_slice x68 -> x0, local copies, waits for them, and re-layouts: 42.3 us -> none  [shards(): lax.scan(down_forward_step, (empty_rows, empty_saved), counters)]
    squeeze x1 -> x0, blocking collectives: 36.3 us -> none  [shards(): far_gain[0]]
    dot_general x12 -> x0, matrix products: 23 us -> none  [the longest x4 8.73 us: layer_forward(): jnp.dot(normed, weight_matrix, preferred_element_type=jnp.float32)]
  transfers between devices with their start and end apart: 88 -> 0, of which waited for: 83 -> 0; matrix products, arithmetic and copies ran while one was open for 9% -> 0% of each run, Pallas kernels for 0% -> 0%
where the time goes in v1:
time: 135 us
  Pallas kernels  132 us (98%)
  local copies, waits for them, and re-layouts  2.19 us (2%)
    pallas_call x1, Pallas kernels, shards(): pl.pallas_call(kernel, out_shape=(jax.ShapeDtypeStruct((1, 64, D), f4), j...  132 us

profile of v1, /device:TPU:1, one launch (start us, length us, event | category | flops | bytes accessed | tf_op | source)
XLA Modules:
  0.0 134.9 jit_solution(7876201473793105508)
XLA Ops:
  0.6 132.1 %shard_map.77 = (f32[1,64,1024]{2,1,0:T(8,128)}, f32[1,64]{1,0:T(1,128)}) custom-call(bf16[2,64,1024]{2,1,0:T(8,128)(2,1)} %down_in.1, bf16[2,64,1024]{2,1,0:T(8,128)(2,1)} %up_in.1, bf16[2,64,1024]{2,1,0:T(8,128)(2,1)} %down_cot.1, bf16[2,64,1024]{2,1,0:T(8,128)(2,1)} %up_cot.1, bf16[1,64,1024]{2,1,0:T(8,128)(2,1)} %w_in.1, bf16[1,64]{1,0:T(2,128)(2,1)} %g_in.1), custom_call_target="tpu_custom_call" | custom-call | tf_op jit(solution)/shard_map/pallas_call | solution.py:546
  132.7 0.0 copy-start
  132.8 1.7 %copy.10 = f32[1,64,1024]{2,1,0:T(8,128)} copy(f32[1,64,1024]{2,1,0:T(8,128)} %get-tuple-element.4) | data formatting | bytes 524288
  134.4 0.0 copy-done
  134.4 0.5 copy.11
Async XLA Ops:
  132.7 1.7 %copy-start = (f32[1,64]{1,0:T(1,128)S(1)}, f32[1,64]{1,0:T(1,128)}, u32[]{:S(2)}) copy-start(f32[1,64]{1,0:T(1,128)} %get-tuple-element.5) | copy-start | bytes 772

commit v2 on v1

--- a/solution.py
+++ b/solution.py
@@ -12,7 +12,7 @@
 CUBIC = 0.044715
 SLOPE = math.sqrt(2.0 / math.pi)
 MESH = pl.DeviceIdType.MESH
-FIRST_PAIR = 8
+FIRST_PAIR = 2
 D = 1024
 HALF = D // 2
 MB_ROWS = 32

time: 135 us -> 131 us (0.970)
  the two profiles are of different devices: /device:TPU:1 before, /device:TPU:64 now
where the time goes in v2:
time: 131 us
  Pallas kernels  128 us (98%)
  local copies, waits for them, and re-layouts  2.19 us (2%)
    pallas_call x1, Pallas kernels, shards(): pl.pallas_call(kernel, out_shape=(jax.ShapeDtypeStruct((1, 64, D), f4), j...  128 us

profile of v2, /device:TPU:64, one launch (start us, length us, event | category | flops | bytes accessed | tf_op | source)
XLA Modules:
  0.0 131.3 jit_solution(10130752553366553481)
XLA Ops:
  0.6 128.4 %shard_map.77 = (f32[1,64,1024]{2,1,0:T(8,128)}, f32[1,64]{1,0:T(1,128)}) custom-call(bf16[2,64,1024]{2,1,0:T(8,128)(2,1)} %down_in.1, bf16[2,64,1024]{2,1,0:T(8,128)(2,1)} %up_in.1, bf16[2,64,1024]{2,1,0:T(8,128)(2,1)} %down_cot.1, bf16[2,64,1024]{2,1,0:T(8,128)(2,1)} %up_cot.1, bf16[1,64,1024]{2,1,0:T(8,128)(2,1)} %w_in.1, bf16[1,64]{1,0:T(2,128)(2,1)} %g_in.1), custom_call_target="tpu_custom_call" | custom-call | tf_op jit(solution)/shard_map/pallas_call | solution.py:546
  129.1 0.0 copy-start
  129.1 1.7 %copy.10 = f32[1,64,1024]{2,1,0:T(8,128)} copy(f32[1,64,1024]{2,1,0:T(8,128)} %get-tuple-element.4) | data formatting | bytes 524288
  130.7 0.0 copy-done
  130.7 0.5 copy.11
Async XLA Ops:
  129.1 1.7 %copy-start = (f32[1,64]{1,0:T(1,128)S(1)}, f32[1,64]{1,0:T(1,128)}, u32[]{:S(2)}) copy-start(f32[1,64]{1,0:T(1,128)} %get-tuple-element.5) | copy-start | bytes 772

commit v3 on v2

--- a/solution.py
+++ b/solution.py
@@ -12,7 +12,7 @@
 CUBIC = 0.044715
 SLOPE = math.sqrt(2.0 / math.pi)
 MESH = pl.DeviceIdType.MESH
-FIRST_PAIR = 2
+FIRST_PAIR = 4
 D = 1024
 HALF = D // 2
 MB_ROWS = 32
@@ -20,10 +20,9 @@
 
 def kernel(
     down_in, up_in, down_cot, up_cot, w_in, g_in, gw_out, gg_out,
-    w, part, r0, r1a, r1b, s1a, s1b, r2a, r2b, zres, zsend, h, du, xs, sl, rinv, xo, do, cot,
+    w, hs, ds, hx, dx, gs, gr, ft, fr, zres, zsend, xs, sl, rinv, xo, do, cot,
     zx_s, zx_r, a1_s, a1_r, b1_s, b1_r, a2_s, a2_r, b2_s, b2_r, d_s, d_r,
-    fx_s, fx_r, bx_s, bx_r, r0_s, r0_r, r1a_s, r1a_r, r1b_s, r1b_r, r2a_s, r2a_r, r2b_s, r2b_r,
-    zr_s, zr_r,
+    fx_s, fx_r, bx_s, bx_r, h_s, h_r, u_s, u_r, g_s, g_r, f_s, f_r, zr_s, zr_r,
 ):
     sec, dp = lax.axis_index("section"), lax.axis_index("dp")
     z, xh = sec // 2, sec % 2
@@ -57,6 +56,7 @@
 
     barrier = pltpu.get_barrier_semaphore()
     peers = [sibling] + [xdev(k) for k in (1, 2, 3)] + [ydev(k) for k in (1, 2, 3)]
+    peers += [at((x + k) % 4, y, z, other) for k in (1, 2, 3)]
     peers += [zdev(1), zdev(-1)]
     if FIRST_PAIR < 8:
         peers += [zdev(2), zdev(-2)]
@@ -78,12 +78,6 @@
     def blk(p, bx, by, cols):
         return w.at[2 * p + bx // 2, by, bx % 2, c, :, cols]
 
-    def row_of(p, by):
-        return w.at[pl.ds(2 * p, 2), by, :, c, :, A]
-
-    def col_of(p, bx):
-        return w.at[2 * p + bx // 2, :, bx % 2, c, :, B]
-
     def zx():
         ref = w.at[own_l, y, xl, c]
         return send(ref, ref, zx_s, zx_r, zpartner)
@@ -102,19 +96,27 @@
 
     def a2(p, src, k):
         ref = blk(p, (x - src + 4) % 4, y, A)
-        return send(ref, ref, a2_s.at[p, src, k - 1], a2_r.at[p, k - 1], ydev(k))
+        return send(ref, ref, a2_s.at[p, src, k - 1], a2_r.at[p, src, k - 1], ydev(k))
 
     def b2(p, src, k):
         ref = blk(p, x, (y - src + 4) % 4, B)
-        return send(ref, ref, b2_s.at[p, src, k - 1], b2_r.at[p, k - 1], xdev(k))
-
-    def a2_wait(p, k):
-        ref = row_of(p, (y - k + 4) % 4)
-        return send(ref, ref, a2_s.at[p, 0, 0], a2_r.at[p, k - 1], sibling)
-
-    def b2_wait(p, k):
-        ref = col_of(p, (x - k + 4) % 4)
-        return send(ref, ref, b2_s.at[p, 0, 0], b2_r.at[p, k - 1], sibling)
+        return send(ref, ref, b2_s.at[p, src, k - 1], b2_r.at[p, src, k - 1], xdev(k))
+
+    def d_a2(p, src, k):
+        ref = blk(p, (x - src + 4) % 4, (y - k + 4) % 4, A)
+        return send(ref, ref, d_s.at[p, 7 + 3 * src + k - 1], d_r.at[p], sibling)
+
+    def d_b2(p, src, k):
+        ref = blk(p, (x - k + 4) % 4, (y - src + 4) % 4, B)
+        return send(ref, ref, d_s.at[p, 19 + 3 * src + k - 1], d_r.at[p], sibling)
+
+    def a2_wait(p, src, k):
+        ref = blk(p, (x - src + 4) % 4, (y - k + 4) % 4, A)
+        return send(ref, ref, a2_s.at[p, src, k - 1], a2_r.at[p, src, k - 1], sibling)
+
+    def b2_wait(p, src, k):
+        ref = blk(p, (x - k + 4) % 4, (y - src + 4) % 4, B)
+        return send(ref, ref, b2_s.at[p, src, k - 1], b2_r.at[p, src, k - 1], sibling)
 
     def d_own(p):
         ref = blk(p, x, y, ALL)
@@ -128,14 +130,6 @@
         ref = blk(p, x, (y - k + 4) % 4, B)
         return send(ref, ref, d_s.at[p, 3 + k], d_r.at[p], sibling)
 
-    def d_a2(p, k):
-        ref = row_of(p, (y - k + 4) % 4)
-        return send(ref, ref, d_s.at[p, 6 + k], d_r.at[p], sibling)
-
-    def d_b2(p, k):
-        ref = col_of(p, (x - k + 4) % 4)
-        return send(ref, ref, d_s.at[p, 9 + k], d_r.at[p], sibling)
-
     def d_wait(p):
         ref = w.at[pl.ds(2 * p, 2), :, :, other]
         return send(ref, ref, d_s.at[p, 0], d_r.at[p], sibling)
@@ -154,35 +148,38 @@
         def _():
             zx_other().wait_recv()
 
-        for k in K:
+        d_own(p).start()
+        for k in (1, 3):
             a1(p, k).start()
             b1(p, k).start()
-        for k in K:
+        a1(p, 2).start()
+        b1(p, 2).start()
+        for k in (1, 3, 2):
             a2(p, 0, k).start()
             b2(p, 0, k).start()
-        d_own(p).start()
         return carry
 
     def gather_mid(i, carry):
         p = (own_p + i) % planes
         for src in (1, 3, 2):
             a1(p, src).wait_recv()
-            for k in K:
+            for k in (1, 3, 2):
                 a2(p, src, k).start()
             d_a1(p, src).start()
             b1(p, src).wait_recv()
-            for k in K:
+            for k in (1, 3, 2):
                 b2(p, src, k).start()
             d_b1(p, src).start()
         return carry
 
     def gather_end(i, carry):
         p = (own_p + i) % planes
-        for k in (1, 3, 2):
-            a2_wait(p, k).wait_recv()
-            d_a2(p, k).start()
-            b2_wait(p, k).wait_recv()
-            d_b2(p, k).start()
+        for src in (0, 1, 3, 2):
+            for k in (1, 3, 2):
+                a2_wait(p, src, k).wait_recv()
+                d_a2(p, src, k).start()
+                b2_wait(p, src, k).wait_recv()
+                d_b2(p, src, k).start()
         return carry
 
     def gather_wait(i, carry):
@@ -222,10 +219,6 @@
     def _():
         load_rows(cot, down_cot, up_cot)
 
-    if FIRST_PAIR < 8:
-        h[...] = jnp.zeros_like(h)
-        du[...] = jnp.zeros_like(du)
-
     lax.fori_loop(0, planes, gather_mid, 0)
     lax.fori_loop(0, planes, gather_end, 0)
     lax.fori_loop(0, planes, gather_wait, 0)
@@ -266,6 +259,34 @@
     def bx_wait(j):
         return send(do.at[j], cot.at[j], bx_s.at[j], bx_r.at[j], sibling)
 
+    me8 = x * 2 + c
+
+    def share(src, dst, ss, rs, l, j, t, cc):
+        part = (t, cc)
+        rows = pl.ds(pl.multiple_of(j * MB_ROWS, MB_ROWS), MB_ROWS)
+        q = 2 * t + cc
+        return send(
+            src.at[l, part[0] if src is hs else part[1], rows, :],
+            dst.at[l // 2, me8, rows, :],
+            ss.at[l * slots + j, q],
+            rs.at[l // 2, me8],
+            at(2 * (l % 2) + t, y, z, cc),
+        )
+
+    def for_owners(l, act):
+        for t in range(2):
+            for cc in range(2):
+
+                @pl.when(jnp.logical_or(2 * (l % 2) + t != x, cc != c))
+                def _(t=t, cc=cc):
+                    act(t, cc)
+
+    def share_h(l, j, t, cc):
+        return share(hs, hx, h_s, h_r, l, j, t, cc)
+
+    def share_u(l, j, t, cc):
+        return share(ds, dx, u_s, u_r, l, j, t, cc)
+
     def forward(j, carry):
         @pl.when(jnp.logical_not(first))
         def _():
@@ -277,7 +298,9 @@
             xf = xs[l, j].astype(jnp.float32)
             r = lax.rsqrt(jnp.mean(xf * xf, axis=-1, keepdims=True) + EPSILON)
             normed = (xf * r).astype(jnp.bfloat16)
-            h[l, rows, :] = normed
+            for t in range(2):
+                for b in range(4):
+                    hs[l, t, rows, b * 128 : (b + 1) * 128] = normed[:, b * 256 + t * 128 : b * 256 + (t + 1) * 128]
             rinv[l, j] = jnp.broadcast_to(r, (MB_ROWS, 128))
             u = jnp.dot(normed, w[l].reshape(D, D), preferred_element_type=jnp.float32)
             u2 = u * u
@@ -297,6 +320,7 @@
                     fx(j).start()
 
             sl[l, j] = 0.5 * (1.0 + t) + 0.5 * u * (1.0 - t * t) * SLOPE * (1.0 + 3.0 * CUBIC * u2)
+            for_owners(l, lambda t, cc: share_h(l, j, t, cc).start())
             return carry
 
         return lax.fori_loop(0, layers, layer, carry)
@@ -314,7 +338,8 @@
             l = layers - 1 - i
             df = cot[j].astype(jnp.float32)
             grad = (df * sl[l, j]).astype(jnp.bfloat16)
-            du[l, rows, :] = grad
+            ds[l, 0, rows, :] = grad[:, 0:HALF]
+            ds[l, 1, rows, :] = grad[:, HALF:D]
 
             @pl.when(jnp.logical_not(jnp.logical_and(first, l == 0)))
             def _():
@@ -334,113 +359,84 @@
                     do[j] = new
                     bx(j).start()
 
+            for_owners(l, lambda t, cc: share_u(l, j, t, cc).start())
             return carry
 
         return lax.fori_loop(0, layers, layer, carry)
 
     lax.fori_loop(0, slots, backward, 0)
-
-    def e0(l):
-        return send(part.at[l, :, :, other], r0.at[l], r0_s.at[l], r0_r.at[l], sibling)
-
-    def e1a(l, k):
-        return send(
-            r0.at[l, (y + k) % 4, :, :, A], r1a.at[l, k - 1], r1a_s.at[l, k - 1], r1a_r.at[l, k - 1], ydev(k)
-        )
-
-    def e1b(l, k):
-        return send(
-            r0.at[l, :, (x + k) % 2, :, B], r1b.at[l // 2, k - 1], r1b_s.at[l, k - 1], r1b_r.at[l // 2, k - 1], xdev(k)
-        )
-
-    def e2a(l, k):
-        return send(
-            s1a.at[l, (x + k) % 2], r2a.at[l // 2, k - 1], r2a_s.at[l, k - 1], r2a_r.at[l // 2, k - 1], xdev(k)
-        )
-
-    def e2b(l, k):
-        p = l // 2
-        return send(
-            s1b.at[p, (y + k) % 4], r2b.at[p, k - 1], r2b_s.at[p, k - 1], r2b_r.at[p, k - 1], ydev(k)
-        )
-
-    def for_x(l, act):
-        for k in K:
-
-            @pl.when(((x + k) % 4) // 2 == l % 2)
-            def _(k=k):
-                act(k)
-
-    def mine(l):
-        return xh == l % 2
 
     def f32(v):
         return v.astype(jnp.float32)
 
-    def reduce_a(i, carry):
-        l = layers - 1 - i
+    def gy(p, k):
+        return send(gs.at[p, (y + k) % 4], gr.at[p, k - 1], g_s.at[p, k - 1], g_r.at[p, k - 1], ydev(k))
+
+    def swap(p):
+        return send(ft.at[p, other], fr.at[p], f_s.at[p], f_r.at[p], sibling)
+
+    def collect(p, count):
+        for src in range(8):
+
+            @pl.when(src != me8)
+            def _(src=src):
+                for ref, rs in ((hx, h_r), (dx, u_r)):
+                    block = ref.at[p, src, pl.ds(0, count), :]
+                    send(block, block, h_s.at[0, 0], rs.at[p, src], sibling).wait_recv()
+
+        l = 2 * p + xh
+        hx[p, me8, 0:count, :] = hs[l, xl, 0:count, :]
+        dx[p, me8, 0:count, :] = ds[l, c, 0:count, :]
         g = lax.dot_general(
-            h[l], du[l], (((0,), (0,)), ((), ())), preferred_element_type=jnp.float32
+            hx[p, :, 0:count, :].reshape(8 * count, HALF),
+            dx[p, :, 0:count, :].reshape(8 * count, HALF),
+            (((0,), (0,)), ((), ())),
+            preferred_element_type=jnp.float32,
         )
-        part[l] = g.astype(jnp.bfloat16).reshape(4, 2, 2, 64, D)
-        e0(l).start()
-        return carry
-
-    def reduce_b(i, carry):
-        l = layers - 1 - i
-        e0(l).wait_recv()
-        r0[l] = (f32(r0[l]) + f32(part[l, :, :, c])).astype(jnp.bfloat16)
-        for k in K:
-            e1a(l, k).start()
-        for_x(l, lambda k: e1b(l, k).start())
-        return carry
-
-    def reduce_c(i, carry):
-        l = layers - 1 - i
-        for k in K:
-            e1a(l, k).wait_recv()
-        s1a[l] = (f32(r0[l, y, :, :, 0:HALF]) + f32(r1a[l, 0]) + f32(r1a[l, 1]) + f32(r1a[l, 2])).astype(jnp.bfloat16)
-        for_x(l, lambda k: e2a(l, k).start())
-
-        @pl.when(mine(l))
-        def _():
-            p = l // 2
-            for k in K:
-                e1b(l, k).wait_recv()
-            s1b[p] = (f32(r0[l, :, xl, :, HALF:D]) + f32(r1b[p, 0]) + f32(r1b[p, 1]) + f32(r1b[p, 2])).astype(jnp.bfloat16)
-            for k in K:
-                e2b(l, k).start()
-
-        return carry
+        gs[p] = g.astype(jnp.bfloat16).reshape(4, 128, HALF)
+        for k in (1, 3, 2):
+            gy(p, k).start()
+
+    def add_up(p):
+        for k in (1, 3, 2):
+            gy(p, k).wait_recv()
+        ft[p] = (f32(gs[p, y]) + f32(gr[p, 0]) + f32(gr[p, 1]) + f32(gr[p, 2])).reshape(2, 64, HALF)
+        swap(p).start()
+
+    here = pl.ds(pl.multiple_of(c * HALF, HALF), HALF)
+    there = pl.ds(pl.multiple_of(other * HALF, HALF), HALF)
 
     def zr():
         return send(zsend, zres, zr_s, zr_r, zpartner)
 
-    def total(l):
-        p = l // 2
-        for k in K:
-            e2a(l, k).wait_recv()
-            e2b(l, k).wait_recv()
-        left = f32(s1a[l, xl]) + f32(r2a[p, 0]) + f32(r2a[p, 1]) + f32(r2a[p, 2])
-        right = f32(s1b[p, y]) + f32(r2b[p, 0]) + f32(r2b[p, 1]) + f32(r2b[p, 2])
-        return left, right
-
-    lax.fori_loop(0, layers, reduce_a, 0)
-    lax.fori_loop(0, layers, reduce_b, 0)
-    lax.fori_loop(0, layers, reduce_c, 0)
+    if FIRST_PAIR > 0:
+
+        @pl.when(single)
+        def _():
+            collect(0, 4 * MB_ROWS)
 
     if FIRST_PAIR < 8:
 
         @pl.when(pair)
         def _():
-            left, right = total(2 * (1 - own_p) + xh)
-            zsend[:, 0:HALF] = left
-            zsend[:, HALF:D] = right
+            collect(1 - own_p, 2 * MB_ROWS)
+            collect(own_p, 2 * MB_ROWS)
+            add_up(1 - own_p)
+
+    add_up(own_p)
+    if FIRST_PAIR < 8:
+
+        @pl.when(pair)
+        def _():
+            p = 1 - own_p
+            swap(p).wait_recv()
+            zsend[:, here] = ft[p, c]
+            zsend[:, there] = fr[p]
             zr().start()
 
-    left, right = total(own_l)
-    gw_out[0, :, 0:HALF] = left
-    gw_out[0, :, HALF:D] = right
+    swap(own_p).wait_recv()
+    gw_out[0, :, here] = ft[own_p, c]
+    gw_out[0, :, there] = fr[own_p]
     if FIRST_PAIR < 8:
 
         @pl.when(pair)
@@ -468,10 +464,10 @@
             for src in range(4):
                 a2(p, src, k).wait_send()
                 b2(p, src, k).wait_send()
+                d_a2(p, src, k).wait_send()
+                d_b2(p, src, k).wait_send()
             d_a1(p, k).wait_send()
             d_b1(p, k).wait_send()
-            d_a2(p, k).wait_send()
-            d_b2(p, k).wait_send()
         d_own(p).wait_send()
         return carry
 
@@ -490,21 +486,23 @@
 
     lax.fori_loop(0, slots, drain_relay, 0)
 
-    def drain_reduce(l, carry):
-        e0(l).wait_send()
+    def drain_layers(l, carry):
+        def drain_rows(j, carry):
+            for_owners(l, lambda t, cc: share_h(l, j, t, cc).wait_send())
+            for_owners(l, lambda t, cc: share_u(l, j, t, cc).wait_send())
+            return carry
+
+        return lax.fori_loop(0, slots, drain_rows, carry)
+
+    lax.fori_loop(0, layers, drain_layers, 0)
+
+    def drain_sums(p, carry):
         for k in K:
-            e1a(l, k).wait_send()
-        for_x(l, lambda k: e1b(l, k).wait_send())
-        for_x(l, lambda k: e2a(l, k).wait_send())
-
-        @pl.when(mine(l))
-        def _():
-            for k in K:
-                e2b(l, k).wait_send()
-
-        return carry
-
-    lax.fori_loop(0, layers, drain_reduce, 0)
+            gy(p, k).wait_send()
+        swap(p).wait_send()
+        return carry
+
+    lax.fori_loop(0, planes, drain_sums, 0)
 
 
 def shards(down_input, up_input, down_cot, up_cot, weight, gain):
@@ -514,18 +512,16 @@
     dma = pltpu.SemaphoreType.DMA
     scratch = [
         pltpu.VMEM((nl, 4, 2, 2, 64, D), bf),
-        pltpu.VMEM((nl, 4, 2, 2, 64, D), bf),
-        pltpu.VMEM((nl, 4, 2, 64, D), bf),
-        pltpu.VMEM((nl, 3, 2, 64, HALF), bf),
-        pltpu.VMEM((np_, 3, 4, 64, HALF), bf),
-        pltpu.VMEM((nl, 2, 64, HALF), bf),
-        pltpu.VMEM((np_, 4, 64, HALF), bf),
-        pltpu.VMEM((np_, 3, 64, HALF), bf),
-        pltpu.VMEM((np_, 3, 64, HALF), bf),
+        pltpu.VMEM((nl, 2, 4 * MB_ROWS, HALF), bf),
+        pltpu.VMEM((nl, 2, 4 * MB_ROWS, HALF), bf),
+        pltpu.VMEM((np_, 8, 4 * MB_ROWS, HALF), bf),
+        pltpu.VMEM((np_, 8, 4 * MB_ROWS, HALF), bf),
+        pltpu.VMEM((np_, 4, 128, HALF), bf),
+        pltpu.VMEM((np_, 3, 128, HALF), bf),
+        pltpu.VMEM((np_, 2, 64, HALF), f4),
+        pltpu.VMEM((np_, 64, HALF), f4),
         pltpu.VMEM((64, D), f4),
         pltpu.VMEM((64, D), f4),
-        pltpu.VMEM((nl, 4 * MB_ROWS, D), bf),
-        pltpu.VMEM((nl, 4 * MB_ROWS, D), bf),
         pltpu.VMEM((nl, 4, MB_ROWS, D), bf),
         pltpu.VMEM((nl, 4, MB_ROWS, D), f4),
         pltpu.VMEM((nl, 4, MB_ROWS, 128), f4),
@@ -534,12 +530,11 @@
         pltpu.VMEM((4, MB_ROWS, D), bf),
         dma, dma,
         dma((np_, 3)), dma((np_, 3)), dma((np_, 3)), dma((np_, 3)),
-        dma((np_, 4, 3)), dma((np_, 3)), dma((np_, 4, 3)), dma((np_, 3)),
-        dma((np_, 13)), dma((np_,)),
+        dma((np_, 4, 3)), dma((np_, 4, 3)), dma((np_, 4, 3)), dma((np_, 4, 3)),
+        dma((np_, 31)), dma((np_,)),
         dma((4,)), dma((4,)), dma((4,)), dma((4,)),
-        dma((nl,)), dma((nl,)),
-        dma((nl, 3)), dma((nl, 3)), dma((nl, 3)), dma((np_, 3)),
-        dma((nl, 3)), dma((np_, 3)), dma((np_, 3)), dma((np_, 3)),
+        dma((8, 4)), dma((np_, 8)), dma((8, 4)), dma((np_, 8)),
+        dma((np_, 3)), dma((np_, 3)), dma((np_,)), dma((np_,)),
         dma, dma,
     ]
     vmem = pl.BlockSpec(memory_space=pltpu.VMEM)

time: 131 us -> 118 us (0.901)
  the two profiles are of different devices: /device:TPU:64 before, /device:TPU:1 now
where the time goes in v3:
time: 118 us
  Pallas kernels  115 us (97%)
  local copies, waits for them, and re-layouts  2.19 us (2%)
    pallas_call x1, Pallas kernels, shards(): pl.pallas_call(kernel, out_shape=(jax.ShapeDtypeStruct((1, 64, D), f4), j...  115 us

profile of v3, /device:TPU:1, one launch (start us, length us, event | category | flops | bytes accessed | tf_op | source)
XLA Modules:
  0.0 118.3 jit_solution(6412721715876962187)
XLA Ops:
  0.6 115.4 %shard_map.77 = (f32[1,64,1024]{2,1,0:T(8,128)}, f32[1,64]{1,0:T(1,128)}) custom-call(bf16[2,64,1024]{2,1,0:T(8,128)(2,1)} %down_in.1, bf16[2,64,1024]{2,1,0:T(8,128)(2,1)} %up_in.1, bf16[2,64,1024]{2,1,0:T(8,128)(2,1)} %down_cot.1, bf16[2,64,1024]{2,1,0:T(8,128)(2,1)} %up_cot.1, bf16[1,64,1024]{2,1,0:T(8,128)(2,1)} %w_in.1, bf16[1,64]{1,0:T(2,128)(2,1)} %g_in.1), custom_call_target="tpu_custom_call" | custom-call | tf_op jit(solution)/shard_map/pallas_call | solution.py:541
  116.1 0.0 copy-start
  116.1 1.7 %copy.10 = f32[1,64,1024]{2,1,0:T(8,128)} copy(f32[1,64,1024]{2,1,0:T(8,128)} %get-tuple-element.4) | data formatting | bytes 524288
  117.8 0.0 copy-done
  117.8 0.5 copy.11
Async XLA Ops:
  116.1 1.7 %copy-start = (f32[1,64]{1,0:T(1,128)S(1)}, f32[1,64]{1,0:T(1,128)}, u32[]{:S(2)}) copy-start(f32[1,64]{1,0:T(1,128)} %get-tuple-element.5) | copy-start | bytes 772

commit v4 on v3

--- a/solution.py
+++ b/solution.py
@@ -20,9 +20,9 @@
 
 def kernel(
     down_in, up_in, down_cot, up_cot, w_in, g_in, gw_out, gg_out,
-    w, hs, ds, hx, dx, gs, gr, ft, fr, zres, zsend, xs, sl, rinv, xo, do, cot,
+    w, wt, hs, ds, hx, dx, acc, gs, gr, ft, fr, zres, zsend, xs, sl, rinv, xo, do, cot,
     zx_s, zx_r, a1_s, a1_r, b1_s, b1_r, a2_s, a2_r, b2_s, b2_r, d_s, d_r,
-    fx_s, fx_r, bx_s, bx_r, h_s, h_r, u_s, u_r, g_s, g_r, f_s, f_r, zr_s, zr_r,
+    fx_s, fx_r, bx_s, bx_r, h_s, h_r, u_s, u_r, g_s, g_r, f_s, f_r, zr_s, zr_r, above,
 ):
     sec, dp = lax.axis_index("section"), lax.axis_index("dp")
     z, xh = sec // 2, sec % 2
@@ -57,11 +57,20 @@
     barrier = pltpu.get_barrier_semaphore()
     peers = [sibling] + [xdev(k) for k in (1, 2, 3)] + [ydev(k) for k in (1, 2, 3)]
     peers += [at((x + k) % 4, y, z, other) for k in (1, 2, 3)]
-    peers += [zdev(1), zdev(-1)]
-    if FIRST_PAIR < 8:
-        peers += [zdev(2), zdev(-2)]
     for peer in peers:
         pl.semaphore_signal(barrier, inc=1, device_id=peer, device_id_type=MESH)
+    for k in (1, 2):
+
+        @pl.when(z + k < 8)
+        def _(k=k):
+            pl.semaphore_signal(barrier, inc=1, device_id=zdev(k), device_id_type=MESH)
+
+    def wait_above():
+        for k in (1, 2):
+
+            @pl.when(z + k < 8)
+            def _(k=k):
+                pl.semaphore_wait(above.at[k - 1], 1)
 
     def send(src, dst, ss, rs, to):
         return pltpu.make_async_remote_copy(
@@ -71,7 +80,13 @@
     eye = lax.broadcasted_iota(jnp.int32, (64, 64), 0) == lax.broadcasted_iota(jnp.int32, (64, 64), 1)
     gain_col = jnp.sum(jnp.where(eye, g_in[...].astype(jnp.float32), 0.0), axis=1, keepdims=True)
     w[own_l, y, xl, c] = (w_in[0].astype(jnp.float32) * gain_col).astype(jnp.bfloat16)
-    pl.semaphore_wait(barrier, len(peers))
+    pl.semaphore_wait(barrier, len(peers) + jnp.minimum(z, 2))
+    for k in (1, 2):
+
+        @pl.when(z >= k)
+        def _(k=k):
+            pl.semaphore_signal(above.at[k - 1], inc=1, device_id=zdev(-k), device_id_type=MESH)
+
 
     A, B, ALL = pl.ds(0, HALF), pl.ds(HALF, HALF), pl.ds(0, D)
 
@@ -139,6 +154,7 @@
 
         @pl.when(pair)
         def _():
+            wait_above()
             zx().start()
 
     def gather_start(i, carry):
@@ -267,9 +283,9 @@
         q = 2 * t + cc
         return send(
             src.at[l, part[0] if src is hs else part[1], rows, :],
-            dst.at[l // 2, me8, rows, :],
+            dst.at[l // 2, j, me8],
             ss.at[l * slots + j, q],
-            rs.at[l // 2, me8],
+            rs.at[l // 2, j, me8],
             at(2 * (l % 2) + t, y, z, cc),
         )
 
@@ -325,7 +341,26 @@
 
         return lax.fori_loop(0, layers, layer, carry)
 
+    def turn(l, carry):
+        wt[l] = w[l].reshape(D, D).T
+        return carry
+
+    @pl.when(last)
+    def _():
+        lax.fori_loop(0, layers, turn, 0)
+
+    if FIRST_PAIR > 0:
+
+        @pl.when(single)
+        def _():
+            wait_above()
+
     lax.fori_loop(0, slots, forward, 0)
+
+    @pl.when(jnp.logical_not(last))
+    def _():
+        lax.fori_loop(0, layers, turn, 0)
+
 
     def backward(j, carry):
         @pl.when(jnp.logical_not(last))
@@ -343,9 +378,7 @@
 
             @pl.when(jnp.logical_not(jnp.logical_and(first, l == 0)))
             def _():
-                a = lax.dot_general(
-                    grad, w[l].reshape(D, D), (((1,), (1,)), ((), ())), preferred_element_type=jnp.float32
-                )
+                a = jnp.dot(grad, wt[l], preferred_element_type=jnp.float32)
                 r = rinv[l, j][:, 0:1]
                 xr = xs[l, j].astype(jnp.float32) * r
                 new = (df + r * (a - xr * jnp.mean(a * xr, axis=-1, keepdims=True))).astype(jnp.bfloat16)
@@ -375,25 +408,32 @@
     def swap(p):
         return send(ft.at[p, other], fr.at[p], f_s.at[p], f_r.at[p], sibling)
 
-    def collect(p, count):
-        for src in range(8):
-
-            @pl.when(src != me8)
-            def _(src=src):
-                for ref, rs in ((hx, h_r), (dx, u_r)):
-                    block = ref.at[p, src, pl.ds(0, count), :]
-                    send(block, block, h_s.at[0, 0], rs.at[p, src], sibling).wait_recv()
-
+    def collect(p):
         l = 2 * p + xh
-        hx[p, me8, 0:count, :] = hs[l, xl, 0:count, :]
-        dx[p, me8, 0:count, :] = ds[l, c, 0:count, :]
-        g = lax.dot_general(
-            hx[p, :, 0:count, :].reshape(8 * count, HALF),
-            dx[p, :, 0:count, :].reshape(8 * count, HALF),
-            (((0,), (0,)), ((), ())),
-            preferred_element_type=jnp.float32,
-        )
-        gs[p] = g.astype(jnp.bfloat16).reshape(4, 128, HALF)
+        acc[...] = jnp.zeros_like(acc)
+
+        def one(j, carry):
+            rows = pl.ds(pl.multiple_of(j * MB_ROWS, MB_ROWS), MB_ROWS)
+            hx[p, j, me8] = hs[l, xl, rows, :]
+            dx[p, j, me8] = ds[l, c, rows, :]
+            for src in range(8):
+
+                @pl.when(src != me8)
+                def _(src=src):
+                    for ref, rs in ((hx, h_r), (dx, u_r)):
+                        block = ref.at[p, j, src]
+                        send(block, block, h_s.at[0, 0], rs.at[p, j, src], sibling).wait_recv()
+
+            acc[...] += lax.dot_general(
+                hx[p, j].reshape(8 * MB_ROWS, HALF),
+                dx[p, j].reshape(8 * MB_ROWS, HALF),
+                (((0,), (0,)), ((), ())),
+                preferred_element_type=jnp.float32,
+            )
+            return carry
+
+        lax.fori_loop(0, slots, one, 0)
+        gs[p] = acc[...].astype(jnp.bfloat16).reshape(4, 128, HALF)
         for k in (1, 3, 2):
             gy(p, k).start()
 
@@ -409,18 +449,17 @@
     def zr():
         return send(zsend, zres, zr_s, zr_r, zpartner)
 
-    if FIRST_PAIR > 0:
-
-        @pl.when(single)
-        def _():
-            collect(0, 4 * MB_ROWS)
-
     if FIRST_PAIR < 8:
 
         @pl.when(pair)
         def _():
-            collect(1 - own_p, 2 * MB_ROWS)
-            collect(own_p, 2 * MB_ROWS)
+            collect(1 - own_p)
+
+    collect(own_p)
+    if FIRST_PAIR < 8:
+
+        @pl.when(pair)
+        def _():
             add_up(1 - own_p)
 
     add_up(own_p)
@@ -512,10 +551,12 @@
     dma = pltpu.SemaphoreType.DMA
     scratch = [
         pltpu.VMEM((nl, 4, 2, 2, 64, D), bf),
+        pltpu.VMEM((nl, D, D), bf),
         pltpu.VMEM((nl, 2, 4 * MB_ROWS, HALF), bf),
         pltpu.VMEM((nl, 2, 4 * MB_ROWS, HALF), bf),
-        pltpu.VMEM((np_, 8, 4 * MB_ROWS, HALF), bf),
-        pltpu.VMEM((np_, 8, 4 * MB_ROWS, HALF), bf),
+        pltpu.VMEM((np_, 4, 8, MB_ROWS, HALF), bf),
+        pltpu.VMEM((np_, 4, 8, MB_ROWS, HALF), bf),
+        pltpu.VMEM((HALF, HALF), f4),
         pltpu.VMEM((np_, 4, 128, HALF), bf),
         pltpu.VMEM((np_, 3, 128, HALF), bf),
         pltpu.VMEM((np_, 2, 64, HALF), f4),
@@ -533,9 +574,10 @@
         dma((np_, 4, 3)), dma((np_, 4, 3)), dma((np_, 4, 3)), dma((np_, 4, 3)),
         dma((np_, 31)), dma((np_,)),
         dma((4,)), dma((4,)), dma((4,)), dma((4,)),
-        dma((8, 4)), dma((np_, 8)), dma((8, 4)), dma((np_, 8)),
+        dma((8, 4)), dma((np_, 4, 8)), dma((8, 4)), dma((np_, 4, 8)),
         dma((np_, 3)), dma((np_, 3)), dma((np_,)), dma((np_,)),
         dma, dma,
+        pltpu.SemaphoreType.REGULAR((2,)),
     ]
     vmem = pl.BlockSpec(memory_space=pltpu.VMEM)
     return pl.pallas_call(

time: 118 us -> 113 us (0.958)
  Pallas kernels: 115 us -> 110 us
    pallas_call x1, Pallas kernels: 115 us -> 110 us  [shards(): pl.pallas_call(kernel, out_shape=(jax.ShapeDtypeStruct((1, 64, D), f4), j...]
where the time goes in v4:
time: 113 us
  Pallas kernels  110 us (97%)
  local copies, waits for them, and re-layouts  2.19 us (2%)
    pallas_call x1, Pallas kernels, shards(): pl.pallas_call(kernel, out_shape=(jax.ShapeDtypeStruct((1, 64, D), f4), j...  110 us

profile of v4, /device:TPU:1, one launch (start us, length us, event | category | flops | bytes accessed | tf_op | source)
XLA Modules:
  0.0 112.9 jit_solution(4037060447599564713)
XLA Ops:
  0.6 110.1 %shard_map.77 = (f32[1,64,1024]{2,1,0:T(8,128)}, f32[1,64]{1,0:T(1,128)}) custom-call(bf16[2,64,1024]{2,1,0:T(8,128)(2,1)} %down_in.1, bf16[2,64,1024]{2,1,0:T(8,128)(2,1)} %up_in.1, bf16[2,64,1024]{2,1,0:T(8,128)(2,1)} %down_cot.1, bf16[2,64,1024]{2,1,0:T(8,128)(2,1)} %up_cot.1, bf16[1,64,1024]{2,1,0:T(8,128)(2,1)} %w_in.1, bf16[1,64]{1,0:T(2,128)(2,1)} %g_in.1), custom_call_target="tpu_custom_call" | custom-call | tf_op jit(solution)/shard_map/pallas_call | solution.py:583
  110.7 0.0 copy-start
  110.7 1.7 %copy.10 = f32[1,64,1024]{2,1,0:T(8,128)} copy(f32[1,64,1024]{2,1,0:T(8,128)} %get-tuple-element.4) | data formatting | bytes 524288
  112.4 0.0 copy-done
  112.4 0.5 copy.11
Async XLA Ops:
  110.7 1.7 %copy-start = (f32[1,64]{1,0:T(1,128)S(1)}, f32[1,64]{1,0:T(1,128)}, u32[]{:S(2)}) copy-start(f32[1,64]{1,0:T(1,128)} %get-tuple-element.5) | copy-start | bytes 772

commit v5 on v4

--- a/solution.py
+++ b/solution.py
@@ -12,7 +12,7 @@
 CUBIC = 0.044715
 SLOPE = math.sqrt(2.0 / math.pi)
 MESH = pl.DeviceIdType.MESH
-FIRST_PAIR = 4
+FIRST_PAIR = 2
 D = 1024
 HALF = D // 2
 MB_ROWS = 32
@@ -20,9 +20,9 @@
 
 def kernel(
     down_in, up_in, down_cot, up_cot, w_in, g_in, gw_out, gg_out,
-    w, wt, hs, ds, hx, dx, acc, gs, gr, ft, fr, zres, zsend, xs, sl, rinv, xo, do, cot,
-    zx_s, zx_r, a1_s, a1_r, b1_s, b1_r, a2_s, a2_r, b2_s, b2_r, d_s, d_r,
-    fx_s, fx_r, bx_s, bx_r, h_s, h_r, u_s, u_r, g_s, g_r, f_s, f_r, zr_s, zr_r, above,
+    wv, w, wt, hs, ds, hx, dx, acc, gs, gr, zres, zsend, xs, sl, rinv, xo, do, cot,
+    zx_s, zx_r, a1_s, a1_r, b1_s, b1_r, a2_s, a2_r, b2_s, b2_r, a3_s, a3_r, b3_s, b3_r, d_s, d_r,
+    fx_s, fx_r, bx_s, bx_r, h_s, h_r, u_s, u_r, g_s, g_r, zr_s, zr_r, above, w_sem, in_sem,
 ):
     sec, dp = lax.axis_index("section"), lax.axis_index("dp")
     z, xh = sec // 2, sec % 2
@@ -54,9 +54,12 @@
     own_l = 2 * own_p + xh
     zpartner = at(x, y, z + 1 - 2 * (z % 2), c)
 
+    load_w = pltpu.make_async_copy(w_in.at[0], wv, w_sem)
+    load_w.start()
     barrier = pltpu.get_barrier_semaphore()
     peers = [sibling] + [xdev(k) for k in (1, 2, 3)] + [ydev(k) for k in (1, 2, 3)]
     peers += [at((x + k) % 4, y, z, other) for k in (1, 2, 3)]
+    peers += [at(x, (y + k) % 4, z, other) for k in (1, 2, 3)]
     for peer in peers:
         pl.semaphore_signal(barrier, inc=1, device_id=peer, device_id_type=MESH)
     for k in (1, 2):
@@ -64,6 +67,12 @@
         @pl.when(z + k < 8)
         def _(k=k):
             pl.semaphore_signal(barrier, inc=1, device_id=zdev(k), device_id_type=MESH)
+
+    if FIRST_PAIR < 8:
+
+        @pl.when(odd == 1)
+        def _():
+            pl.semaphore_signal(barrier, inc=1, device_id=zpartner, device_id_type=MESH)
 
     def wait_above():
         for k in (1, 2):
@@ -79,8 +88,9 @@
 
     eye = lax.broadcasted_iota(jnp.int32, (64, 64), 0) == lax.broadcasted_iota(jnp.int32, (64, 64), 1)
     gain_col = jnp.sum(jnp.where(eye, g_in[...].astype(jnp.float32), 0.0), axis=1, keepdims=True)
-    w[own_l, y, xl, c] = (w_in[0].astype(jnp.float32) * gain_col).astype(jnp.bfloat16)
-    pl.semaphore_wait(barrier, len(peers) + jnp.minimum(z, 2))
+    load_w.wait()
+    w[own_l, y, xl, c] = (wv[...].astype(jnp.float32) * gain_col).astype(jnp.bfloat16)
+    pl.semaphore_wait(barrier, len(peers) + jnp.minimum(z, 2) + (ispair - odd))
     for k in (1, 2):
 
         @pl.when(z >= k)
@@ -111,27 +121,54 @@
 
     def a2(p, src, k):
         ref = blk(p, (x - src + 4) % 4, y, A)
-        return send(ref, ref, a2_s.at[p, src, k - 1], a2_r.at[p, src, k - 1], ydev(k))
+        return send(ref, ref, a2_s.at[p, src, k // 2], a2_r.at[p, src, k // 2], ydev(k))
 
     def b2(p, src, k):
         ref = blk(p, x, (y - src + 4) % 4, B)
-        return send(ref, ref, b2_s.at[p, src, k - 1], b2_r.at[p, src, k - 1], xdev(k))
+        return send(ref, ref, b2_s.at[p, src, k // 2], b2_r.at[p, src, k // 2], xdev(k))
+
+    def half_blk(p, bx, by, cols, k):
+        return w.at[2 * p + bx // 2, by, bx % 2, c, pl.ds(32 * (k // 2), 32), cols]
+
+    def a3(p, src, k):
+        ref = half_blk(p, (x - src + 4) % 4, (y - k + 4) % 4, A, k)
+        return send(ref, ref, a3_s.at[p, src, k // 2], a3_r.at[p, src, k // 2], ydev(k))
+
+    def b3(p, src, k):
+        ref = half_blk(p, (x - k + 4) % 4, (y - src + 4) % 4, B, k)
+        return send(ref, ref, b3_s.at[p, src, k // 2], b3_r.at[p, src, k // 2], xdev(k))
+
+    def a3_wait(p, src, k):
+        ref = half_blk(p, (x - src + 4) % 4, (y + 2) % 4, A, k)
+        return send(ref, ref, a3_s.at[p, src, k // 2], a3_r.at[p, src, k // 2], sibling)
+
+    def b3_wait(p, src, k):
+        ref = half_blk(p, (x + 2) % 4, (y - src + 4) % 4, B, k)
+        return send(ref, ref, b3_s.at[p, src, k // 2], b3_r.at[p, src, k // 2], sibling)
 
     def d_a2(p, src, k):
         ref = blk(p, (x - src + 4) % 4, (y - k + 4) % 4, A)
-        return send(ref, ref, d_s.at[p, 7 + 3 * src + k - 1], d_r.at[p], sibling)
+        return send(ref, ref, d_s.at[p, 7 + 2 * src + k // 2], d_r.at[p], sibling)
 
     def d_b2(p, src, k):
         ref = blk(p, (x - k + 4) % 4, (y - src + 4) % 4, B)
-        return send(ref, ref, d_s.at[p, 19 + 3 * src + k - 1], d_r.at[p], sibling)
+        return send(ref, ref, d_s.at[p, 15 + 2 * src + k // 2], d_r.at[p], sibling)
+
+    def d_a3(p, src, k):
+        ref = half_blk(p, (x - src + 4) % 4, (y + 2) % 4, A, k)
+        return send(ref, ref, d_s.at[p, 23 + 2 * src + k // 2], d_r.at[p], sibling)
+
+    def d_b3(p, src, k):
+        ref = half_blk(p, (x + 2) % 4, (y - src + 4) % 4, B, k)
+        return send(ref, ref, d_s.at[p, 31 + 2 * src + k // 2], d_r.at[p], sibling)
 
     def a2_wait(p, src, k):
         ref = blk(p, (x - src + 4) % 4, (y - k + 4) % 4, A)
-        return send(ref, ref, a2_s.at[p, src, k - 1], a2_r.at[p, src, k - 1], sibling)
+        return send(ref, ref, a2_s.at[p, src, k // 2], a2_r.at[p, src, k // 2], sibling)
 
     def b2_wait(p, src, k):
         ref = blk(p, (x - k + 4) % 4, (y - src + 4) % 4, B)
-        return send(ref, ref, b2_s.at[p, src, k - 1], b2_r.at[p, src, k - 1], sibling)
+        return send(ref, ref, b2_s.at[p, src, k // 2], b2_r.at[p, src, k // 2], sibling)
 
     def d_own(p):
         ref = blk(p, x, y, ALL)
@@ -149,12 +186,11 @@
         ref = w.at[pl.ds(2 * p, 2), :, :, other]
         return send(ref, ref, d_s.at[p, 0], d_r.at[p], sibling)
 
-    K = (1, 2, 3)
+    K, N = (1, 2, 3), (1, 3)
     if FIRST_PAIR < 8:
 
         @pl.when(pair)
         def _():
-            wait_above()
             zx().start()
 
     def gather_start(i, carry):
@@ -170,32 +206,53 @@
             b1(p, k).start()
         a1(p, 2).start()
         b1(p, 2).start()
-        for k in (1, 3, 2):
+        for k in N:
             a2(p, 0, k).start()
             b2(p, 0, k).start()
         return carry
+
+    def onward(p, src):
+        a1(p, src).wait_recv()
+        for k in N:
+            a2(p, src, k).start()
+        d_a1(p, src).start()
+        b1(p, src).wait_recv()
+        for k in N:
+            b2(p, src, k).start()
+        d_b1(p, src).start()
+
+    def arrived(p, src):
+        for k in N:
+            a2_wait(p, src, k).wait_recv()
+            a3(p, src, k).start()
+            d_a2(p, src, k).start()
+            b2_wait(p, src, k).wait_recv()
+            b3(p, src, k).start()
+            d_b2(p, src, k).start()
+
+    def far_side(p, src):
+        for k in N:
+            a3_wait(p, src, k).wait_recv()
+            d_a3(p, src, k).start()
+            b3_wait(p, src, k).wait_recv()
+            d_b3(p, src, k).start()
 
     def gather_mid(i, carry):
         p = (own_p + i) % planes
         for src in (1, 3, 2):
-            a1(p, src).wait_recv()
-            for k in (1, 3, 2):
-                a2(p, src, k).start()
-            d_a1(p, src).start()
-            b1(p, src).wait_recv()
-            for k in (1, 3, 2):
-                b2(p, src, k).start()
-            d_b1(p, src).start()
+            onward(p, src)
+        arrived(p, 0)
         return carry
 
     def gather_end(i, carry):
         p = (own_p + i) % planes
-        for src in (0, 1, 3, 2):
-            for k in (1, 3, 2):
-                a2_wait(p, src, k).wait_recv()
-                d_a2(p, src, k).start()
-                b2_wait(p, src, k).wait_recv()
-                d_b2(p, src, k).start()
+        arrived(p, 1)
+        arrived(p, 3)
+        far_side(p, 0)
+        arrived(p, 2)
+        far_side(p, 1)
+        far_side(p, 3)
+        far_side(p, 2)
         return carry
 
     def gather_wait(i, carry):
@@ -207,25 +264,22 @@
     first = z < (2 if FIRST_PAIR == 0 else 1)
     last = z >= (7 if FIRST_PAIR == 8 else 6)
 
+    def rows_in(ref, dst, slot, j):
+        rows = pl.ds(pl.multiple_of((j % 2) * MB_ROWS, MB_ROWS), MB_ROWS)
+        return pltpu.make_async_copy(ref.at[j // 2, rows, :], dst.at[slot], in_sem.at[slot])
+
     def load_rows(dst, down, up):
-        for slot in range(4):
-            def take(j, slot=slot):
-                b, half = j // 2, j % 2
-                for ref, cond in ((down, xh == 0), (up, xh == 1)):
-
-                    @pl.when(cond)
-                    def _(ref=ref):
-                        dst[slot] = ref[b, pl.ds(pl.multiple_of(half * MB_ROWS, MB_ROWS), MB_ROWS), :]
-
-            if FIRST_PAIR == 8:
-                take(slot)
-            elif slot < 2:
-                take((2 * slot + odd) if FIRST_PAIR == 0 else slot * planes + odd)
-            else:
-
-                @pl.when(single)
-                def _(slot=slot):
-                    take(slot)
+        def one(slot, carry):
+            j = slot * planes + odd
+            for ref, cond in ((down, xh == 0), (up, xh == 1)):
+
+                @pl.when(cond)
+                def _(ref=ref):
+                    rows_in(ref, dst, slot, j).start()
+
+            return carry
+
+        lax.fori_loop(0, slots, one, 0)
 
     @pl.when(first)
     def _():
@@ -304,6 +358,10 @@
         return share(ds, dx, u_s, u_r, l, j, t, cc)
 
     def forward(j, carry):
+        @pl.when(first)
+        def _():
+            rows_in(down_in, xs.at[0], j, 0).wait()
+
         @pl.when(jnp.logical_not(first))
         def _():
             fx_wait(j).wait_recv()
@@ -349,12 +407,7 @@
     def _():
         lax.fori_loop(0, layers, turn, 0)
 
-    if FIRST_PAIR > 0:
-
-        @pl.when(single)
-        def _():
-            wait_above()
-
+    wait_above()
     lax.fori_loop(0, slots, forward, 0)
 
     @pl.when(jnp.logical_not(last))
@@ -363,6 +416,10 @@
 
 
     def backward(j, carry):
+        @pl.when(last)
+        def _():
+            rows_in(down_cot, cot, j, 0).wait()
+
         @pl.when(jnp.logical_not(last))
         def _():
             bx_wait(j).wait_recv()
@@ -402,11 +459,24 @@
     def f32(v):
         return v.astype(jnp.float32)
 
-    def gy(p, k):
-        return send(gs.at[p, (y + k) % 4], gr.at[p, k - 1], g_s.at[p, k - 1], g_r.at[p, k - 1], ydev(k))
-
-    def swap(p):
-        return send(ft.at[p, other], fr.at[p], f_s.at[p], f_r.at[p], sibling)
+    def gy(p, k, cc):
+        to_y = (y + k) % 4
+        return send(gs.at[p, to_y, cc], gr.at[p, c, k], g_s.at[p, k, cc], g_r.at[p, c, k], at(x, to_y, z, cc))
+
+    def for_sums(p, act):
+        for k in (1, 3, 2, 0):
+            for cc in range(2):
+                if k == 0:
+
+                    @pl.when(cc != c)
+                    def _(k=k, cc=cc):
+                        act(p, k, cc)
+
+                else:
+                    act(p, k, cc)
+
+    def sum_wait(p, k, cs):
+        return send(gr.at[p, cs, k], gr.at[p, cs, k], g_s.at[p, k, cs], g_r.at[p, cs, k], sibling)
 
     def collect(p):
         l = 2 * p + xh
@@ -433,18 +503,22 @@
             return carry
 
         lax.fori_loop(0, slots, one, 0)
-        gs[p] = acc[...].astype(jnp.bfloat16).reshape(4, 128, HALF)
-        for k in (1, 3, 2):
-            gy(p, k).start()
-
-    def add_up(p):
-        for k in (1, 3, 2):
-            gy(p, k).wait_recv()
-        ft[p] = (f32(gs[p, y]) + f32(gr[p, 0]) + f32(gr[p, 1]) + f32(gr[p, 2])).reshape(2, 64, HALF)
-        swap(p).start()
-
-    here = pl.ds(pl.multiple_of(c * HALF, HALF), HALF)
-    there = pl.ds(pl.multiple_of(other * HALF, HALF), HALF)
+        gs[p] = acc[...].astype(jnp.bfloat16).reshape(4, 2, 64, HALF)
+        for_sums(p, lambda p, k, cc: gy(p, k, cc).start())
+        gr[p, c, 0] = gs[p, y, c]
+
+    def add_up(p, out):
+        for cs in range(2):
+
+            @pl.when(cs != c)
+            def _(cs=cs):
+                sum_wait(p, 0, cs).wait_recv()
+
+            for k in (1, 3, 2):
+                sum_wait(p, k, cs).wait_recv()
+            out[:, cs * HALF : (cs + 1) * HALF] = (
+                f32(gr[p, cs, 0]) + f32(gr[p, cs, 1]) + f32(gr[p, cs, 2]) + f32(gr[p, cs, 3])
+            )
 
     def zr():
         return send(zsend, zres, zr_s, zr_r, zpartner)
@@ -460,22 +534,10 @@
 
         @pl.when(pair)
         def _():
-            add_up(1 - own_p)
-
-    add_up(own_p)
-    if FIRST_PAIR < 8:
-
-        @pl.when(pair)
-        def _():
-            p = 1 - own_p
-            swap(p).wait_recv()
-            zsend[:, here] = ft[p, c]
-            zsend[:, there] = fr[p]
+            add_up(1 - own_p, zsend)
             zr().start()
 
-    swap(own_p).wait_recv()
-    gw_out[0, :, here] = ft[own_p, c]
-    gw_out[0, :, there] = fr[own_p]
+    add_up(own_p, gw_out.at[0])
     if FIRST_PAIR < 8:
 
         @pl.when(pair)
@@ -484,7 +546,7 @@
             gw_out[0] = gw_out[0] + zres[...]
 
     full = gw_out[0]
-    per_row = jnp.sum(full * w_in[0].astype(jnp.float32), axis=1, keepdims=True)
+    per_row = jnp.sum(full * wv[...].astype(jnp.float32), axis=1, keepdims=True)
     gg_out[...] = jnp.sum(jnp.where(eye, per_row, 0.0), axis=0, keepdims=True)
     gw_out[0] = full * gain_col
 
@@ -500,13 +562,12 @@
         for k in K:
             a1(p, k).wait_send()
             b1(p, k).wait_send()
-            for src in range(4):
-                a2(p, src, k).wait_send()
-                b2(p, src, k).wait_send()
-                d_a2(p, src, k).wait_send()
-                d_b2(p, src, k).wait_send()
             d_a1(p, k).wait_send()
             d_b1(p, k).wait_send()
+        for src in range(4):
+            for k in N:
+                for copy in (a2, b2, a3, b3, d_a2, d_b2, d_a3, d_b3):
+                    copy(p, src, k).wait_send()
         d_own(p).wait_send()
         return carry
 
@@ -536,9 +597,7 @@
     lax.fori_loop(0, layers, drain_layers, 0)
 
     def drain_sums(p, carry):
-        for k in K:
-            gy(p, k).wait_send()
-        swap(p).wait_send()
+        for_sums(p, lambda p, k, cc: gy(p, k, cc).wait_send())
         return carry
 
     lax.fori_loop(0, planes, drain_sums, 0)
@@ -550,6 +609,7 @@
     bf, f4 = jnp.bfloat16, jnp.float32
     dma = pltpu.SemaphoreType.DMA
     scratch = [
+        pltpu.VMEM((64, D), bf),
         pltpu.VMEM((nl, 4, 2, 2, 64, D), bf),
         pltpu.VMEM((nl, D, D), bf),
         pltpu.VMEM((nl, 2, 4 * MB_ROWS, HALF), bf),
@@ -557,10 +617,8 @@
         pltpu.VMEM((np_, 4, 8, MB_ROWS, HALF), bf),
         pltpu.VMEM((np_, 4, 8, MB_ROWS, HALF), bf),
         pltpu.VMEM((HALF, HALF), f4),
-        pltpu.VMEM((np_, 4, 128, HALF), bf),
-        pltpu.VMEM((np_, 3, 128, HALF), bf),
-        pltpu.VMEM((np_, 2, 64, HALF), f4),
-        pltpu.VMEM((np_, 64, HALF), f4),
+        pltpu.VMEM((np_, 4, 2, 64, HALF), bf),
+        pltpu.VMEM((np_, 2, 4, 64, HALF), bf),
         pltpu.VMEM((64, D), f4),
         pltpu.VMEM((64, D), f4),
         pltpu.VMEM((nl, 4, MB_ROWS, D), bf),
@@ -571,13 +629,15 @@
         pltpu.VMEM((4, MB_ROWS, D), bf),
         dma, dma,
         dma((np_, 3)), dma((np_, 3)), dma((np_, 3)), dma((np_, 3)),
-        dma((np_, 4, 3)), dma((np_, 4, 3)), dma((np_, 4, 3)), dma((np_, 4, 3)),
-        dma((np_, 31)), dma((np_,)),
+        dma((np_, 4, 2)), dma((np_, 4, 2)), dma((np_, 4, 2)), dma((np_, 4, 2)),
+        dma((np_, 4, 2)), dma((np_, 4, 2)), dma((np_, 4, 2)), dma((np_, 4, 2)),
+        dma((np_, 39)), dma((np_,)),
         dma((4,)), dma((4,)), dma((4,)), dma((4,)),
         dma((8, 4)), dma((np_, 4, 8)), dma((8, 4)), dma((np_, 4, 8)),
-        dma((np_, 3)), dma((np_, 3)), dma((np_,)), dma((np_,)),
+        dma((np_, 4, 2)), dma((np_, 2, 4)),
         dma, dma,
         pltpu.SemaphoreType.REGULAR((2,)),
+        dma, dma((4,)),
     ]
     vmem = pl.BlockSpec(memory_space=pltpu.VMEM)
     return pl.pallas_call(
@@ -586,7 +646,7 @@
             jax.ShapeDtypeStruct((1, 64, D), f4),
             jax.ShapeDtypeStruct((1, 64), f4),
         ),
-        in_specs=[vmem] * 6,
+        in_specs=[pl.BlockSpec(memory_space=pl.ANY)] * 5 + [vmem],
         out_specs=(vmem, vmem),
         scratch_shapes=scratch,
         compiler_params=pltpu.CompilerParams(

time: 113 us -> 109 us (0.965)
  Pallas kernels: 110 us -> 106 us
    pallas_call x1, Pallas kernels: 110 us -> 106 us  [shards(): pl.pallas_call(kernel, out_shape=(jax.ShapeDtypeStruct((1, 64, D), f4), j...]
where the time goes in v5:
time: 109 us
  Pallas kernels  106 us (97%)
  local copies, waits for them, and re-layouts  2.19 us (2%)
    pallas_call x1, Pallas kernels, shards(): pl.pallas_call(kernel, out_shape=(jax.ShapeDtypeStruct((1, 64, D), f4), j...  106 us
    unnamed x4, local copies, waits for them, and re-layouts  2.19 us

profile of v5, /device:TPU:1, one launch (start us, length us, event | category | flops | bytes accessed | tf_op | source)
XLA Modules:
  0.0 109.3 jit_solution(13879529250570681026)
XLA Ops:
  0.6 106.5 %shard_map.77 = (f32[1,64,1024]{2,1,0:T(8,128)}, f32[1,64]{1,0:T(1,128)}) custom-call(bf16[2,64,1024]{2,1,0:T(8,128)(2,1)} %down_in.1, bf16[2,64,1024]{2,1,0:T(8,128)(2,1)} %up_in.1, bf16[2,64,1024]{2,1,0:T(8,128)(2,1)} %down_cot.1, bf16[2,64,1024]{2,1,0:T(8,128)(2,1)} %up_cot.1, bf16[1,64,1024]{2,1,0:T(8,128)(2,1)} %w_in.1, bf16[1,64]{1,0:T(2,128)(2,1)} %g_in.1), custom_call_target="tpu_custom_call" | custom-call | tf_op jit(solution)/shard_map/pallas_call | solution.py:643
  107.1 0.0 copy-start
  107.1 1.7 %copy.10 = f32[1,64,1024]{2,1,0:T(8,128)} copy(f32[1,64,1024]{2,1,0:T(8,128)} %get-tuple-element.4) | data formatting | bytes 524288
  108.8 0.0 copy-done
  108.8 0.5 copy.11
Async XLA Ops:
  107.1 1.7 %copy-start = (f32[1,64]{1,0:T(1,128)S(1)}, f32[1,64]{1,0:T(1,128)}, u32[]{:S(2)}) copy-start(f32[1,64]{1,0:T(1,128)} %get-tuple-element.5) | copy-start | bytes 772

commit v6 on v5

--- a/solution.py
+++ b/solution.py
@@ -20,9 +20,9 @@
 
 def kernel(
     down_in, up_in, down_cot, up_cot, w_in, g_in, gw_out, gg_out,
-    wv, w, wt, hs, ds, hx, dx, acc, gs, gr, zres, zsend, xs, sl, rinv, xo, do, cot,
+    wv, w, wt, hs, ds, hx, dx, acc, gs, gr, zres, zsend, xs, sl, rinv, do, cot,
     zx_s, zx_r, a1_s, a1_r, b1_s, b1_r, a2_s, a2_r, b2_s, b2_r, a3_s, a3_r, b3_s, b3_r, d_s, d_r,
-    fx_s, fx_r, bx_s, bx_r, h_s, h_r, u_s, u_r, g_s, g_r, zr_s, zr_r, above, w_sem, in_sem,
+    fx_s, fx_r, bx_s, bx_r, h_s, h_r, hf_s, u_s, u_r, g_s, g_r, zr_s, zr_r, above, w_sem, in_sem,
 ):
     sec, dp = lax.axis_index("section"), lax.axis_index("dp")
     z, xh = sec // 2, sec % 2
@@ -40,7 +40,7 @@
         return at(x, (y + k) % 4, z, c)
 
     def zdev(k):
-        return at(x, y, (z + 8 + k) % 8, c)
+        return at(x, y, (z + 8 + k) % 8, other)
 
     sibling = at(x, y, z, other)
     pair = z >= FIRST_PAIR
@@ -60,6 +60,8 @@
     peers = [sibling] + [xdev(k) for k in (1, 2, 3)] + [ydev(k) for k in (1, 2, 3)]
     peers += [at((x + k) % 4, y, z, other) for k in (1, 2, 3)]
     peers += [at(x, (y + k) % 4, z, other) for k in (1, 2, 3)]
+    beside = x + 1 - 2 * xl
+    peers += [at(beside, (y + k) % 4, z, ac) for k in (1, 2, 3) for ac in (0, 1)]
     for peer in peers:
         pl.semaphore_signal(barrier, inc=1, device_id=peer, device_id_type=MESH)
     for k in (1, 2):
@@ -70,7 +72,7 @@
 
     if FIRST_PAIR < 8:
 
-        @pl.when(odd == 1)
+        @pl.when(pair)
         def _():
             pl.semaphore_signal(barrier, inc=1, device_id=zpartner, device_id_type=MESH)
 
@@ -90,7 +92,7 @@
     gain_col = jnp.sum(jnp.where(eye, g_in[...].astype(jnp.float32), 0.0), axis=1, keepdims=True)
     load_w.wait()
     w[own_l, y, xl, c] = (wv[...].astype(jnp.float32) * gain_col).astype(jnp.bfloat16)
-    pl.semaphore_wait(barrier, len(peers) + jnp.minimum(z, 2) + (ispair - odd))
+    pl.semaphore_wait(barrier, len(peers) + jnp.minimum(z, 2) + ispair)
     for k in (1, 2):
 
         @pl.when(z >= k)
@@ -317,10 +319,10 @@
 
     def fx(j):
         to, slot = f_route(j)
-        return send(xo.at[j], xs.at[0, slot], fx_s.at[j], fx_r.at[slot], to)
+        return send(xs.at[layers, j], xs.at[0, slot], fx_s.at[j], fx_r.at[slot], to)
 
     def fx_wait(j):
-        return send(xo.at[j], xs.at[0, j], fx_s.at[j], fx_r.at[j], sibling)
+        return send(xs.at[layers, j], xs.at[0, j], fx_s.at[j], fx_r.at[j], sibling)
 
     def bx(j):
         to, slot = b_route(j)
@@ -331,16 +333,39 @@
 
     me8 = x * 2 + c
 
-    def share(src, dst, ss, rs, l, j, t, cc):
-        part = (t, cc)
-        rows = pl.ds(pl.multiple_of(j * MB_ROWS, MB_ROWS), MB_ROWS)
-        q = 2 * t + cc
+    quarter = 2 * xl + c
+    WIDE = D // 4
+
+    def mb_rows(j):
+        return pl.ds(pl.multiple_of(j * MB_ROWS, MB_ROWS), MB_ROWS)
+
+    def share_h(l, j, t):
+        to_x = 2 * (l % 2) + t
+        near = (to_x == x).astype(jnp.int32)
+        core = c + near * (1 - 2 * c)
         return send(
-            src.at[l, part[0] if src is hs else part[1], rows, :],
-            dst.at[l // 2, j, me8],
-            ss.at[l * slots + j, q],
-            rs.at[l // 2, j, me8],
-            at(2 * (l % 2) + t, y, z, cc),
+            hs.at[l, mb_rows(j), :], hx.at[l // 2, j, me8], h_s.at[l * slots + j, t], h_r.at[l // 2, j, me8],
+            at(to_x, y, z, core),
+        )
+
+    def hand_h(p, j, k):
+        src = ((x + k) % 4) * 2 + c
+        ref = hx.at[p, j, src]
+        return send(ref, ref, hf_s.at[p, j, k - 1], h_r.at[p, j, src], sibling)
+
+    def hand_over(p):
+        def one(j, carry):
+            for k in K:
+                hand_h(p, j, k).wait_recv()
+                hand_h(p, j, k).start()
+            return carry
+
+        lax.fori_loop(0, slots, one, 0)
+
+    def share_u(l, j, t, cc):
+        return send(
+            ds.at[l, 2 * t + cc, mb_rows(j), :], dx.at[l // 2, j, me8], u_s.at[l * slots + j, 2 * t + cc],
+            u_r.at[l // 2, j, me8], at(2 * (l % 2) + t, y, z, cc),
         )
 
     def for_owners(l, act):
@@ -351,11 +376,23 @@
                 def _(t=t, cc=cc):
                     act(t, cc)
 
-    def share_h(l, j, t, cc):
-        return share(hs, hx, h_s, h_r, l, j, t, cc)
-
-    def share_u(l, j, t, cc):
-        return share(ds, dx, u_s, u_r, l, j, t, cc)
+    def f32(v):
+        return v.astype(jnp.float32)
+
+    def forward_layers(j, count):
+        rows = pl.ds(pl.multiple_of(j * MB_ROWS, MB_ROWS), MB_ROWS)
+        xf = f32(xs[0, j])
+        for l in range(count):
+            r = lax.rsqrt(jnp.mean(xf * xf, axis=-1, keepdims=True) + EPSILON)
+            normed = (xf * r).astype(jnp.bfloat16)
+            u = jnp.dot(normed, w[l].reshape(D, D), preferred_element_type=jnp.float32)
+            t = jnp.tanh(SLOPE * (u + CUBIC * (u * u) * u))
+            nxt = (xf + 0.5 * u * (1.0 + t)).astype(jnp.bfloat16)
+            xs[l + 1, j] = nxt
+            xf = f32(nxt)
+            sl[l, j] = u
+            rinv[l, j] = jnp.broadcast_to(r, (MB_ROWS, 128))
+            hs[l, rows, :] = normed
 
     def forward(j, carry):
         @pl.when(first)
@@ -366,196 +403,45 @@
         def _():
             fx_wait(j).wait_recv()
 
-        rows = pl.ds(pl.multiple_of(j * MB_ROWS, MB_ROWS), MB_ROWS)
-
-        def layer(l, carry):
-            xf = xs[l, j].astype(jnp.float32)
-            r = lax.rsqrt(jnp.mean(xf * xf, axis=-1, keepdims=True) + EPSILON)
-            normed = (xf * r).astype(jnp.bfloat16)
-            for t in range(2):
-                for b in range(4):
-                    hs[l, t, rows, b * 128 : (b + 1) * 128] = normed[:, b * 256 + t * 128 : b * 256 + (t + 1) * 128]
-            rinv[l, j] = jnp.broadcast_to(r, (MB_ROWS, 128))
-            u = jnp.dot(normed, w[l].reshape(D, D), preferred_element_type=jnp.float32)
+        if FIRST_PAIR > 0:
+
+            @pl.when(single)
+            def _():
+                forward_layers(j, 2)
+
+        if FIRST_PAIR < 8:
+
+            @pl.when(pair)
+            def _():
+                forward_layers(j, 4)
+
+        @pl.when(jnp.logical_not(last))
+        def _():
+            fx(j).start()
+
+        return carry
+
+    def slopes(l, carry):
+        def one(j, carry):
+            u = sl[l, j]
             u2 = u * u
             t = jnp.tanh(SLOPE * (u + CUBIC * u2 * u))
-            nxt = (xf + 0.5 * u * (1.0 + t)).astype(jnp.bfloat16)
-
-            @pl.when(l < layers - 1)
-            def _():
-                xs[l + 1, j] = nxt
-
-            @pl.when(l == layers - 1)
-            def _():
-                xo[j] = nxt
-
-                @pl.when(jnp.logical_not(last))
-                def _():
-                    fx(j).start()
-
             sl[l, j] = 0.5 * (1.0 + t) + 0.5 * u * (1.0 - t * t) * SLOPE * (1.0 + 3.0 * CUBIC * u2)
-            for_owners(l, lambda t, cc: share_h(l, j, t, cc).start())
-            return carry
-
-        return lax.fori_loop(0, layers, layer, carry)
+            return carry
+
+        return lax.fori_loop(0, slots, one, carry)
 
     def turn(l, carry):
         wt[l] = w[l].reshape(D, D).T
         return carry
 
-    @pl.when(last)
-    def _():
-        lax.fori_loop(0, layers, turn, 0)
-
-    wait_above()
-    lax.fori_loop(0, slots, forward, 0)
-
-    @pl.when(jnp.logical_not(last))
-    def _():
-        lax.fori_loop(0, layers, turn, 0)
-
-
-    def backward(j, carry):
-        @pl.when(last)
-        def _():
-            rows_in(down_cot, cot, j, 0).wait()
-
-        @pl.when(jnp.logical_not(last))
-        def _():
-            bx_wait(j).wait_recv()
-
-        rows = pl.ds(pl.multiple_of(j * MB_ROWS, MB_ROWS), MB_ROWS)
-
-        def layer(i, carry):
-            l = layers - 1 - i
-            df = cot[j].astype(jnp.float32)
-            grad = (df * sl[l, j]).astype(jnp.bfloat16)
-            ds[l, 0, rows, :] = grad[:, 0:HALF]
-            ds[l, 1, rows, :] = grad[:, HALF:D]
-
-            @pl.when(jnp.logical_not(jnp.logical_and(first, l == 0)))
-            def _():
-                a = jnp.dot(grad, wt[l], preferred_element_type=jnp.float32)
-                r = rinv[l, j][:, 0:1]
-                xr = xs[l, j].astype(jnp.float32) * r
-                new = (df + r * (a - xr * jnp.mean(a * xr, axis=-1, keepdims=True))).astype(jnp.bfloat16)
-
-                @pl.when(l > 0)
-                def _():
-                    cot[j] = new
-
-                @pl.when(l == 0)
-                def _():
-                    do[j] = new
-                    bx(j).start()
-
-            for_owners(l, lambda t, cc: share_u(l, j, t, cc).start())
-            return carry
-
-        return lax.fori_loop(0, layers, layer, carry)
-
-    lax.fori_loop(0, slots, backward, 0)
-
-    def f32(v):
-        return v.astype(jnp.float32)
-
-    def gy(p, k, cc):
-        to_y = (y + k) % 4
-        return send(gs.at[p, to_y, cc], gr.at[p, c, k], g_s.at[p, k, cc], g_r.at[p, c, k], at(x, to_y, z, cc))
-
-    def for_sums(p, act):
-        for k in (1, 3, 2, 0):
-            for cc in range(2):
-                if k == 0:
-
-                    @pl.when(cc != c)
-                    def _(k=k, cc=cc):
-                        act(p, k, cc)
-
-                else:
-                    act(p, k, cc)
-
-    def sum_wait(p, k, cs):
-        return send(gr.at[p, cs, k], gr.at[p, cs, k], g_s.at[p, k, cs], g_r.at[p, cs, k], sibling)
-
-    def collect(p):
-        l = 2 * p + xh
-        acc[...] = jnp.zeros_like(acc)
-
+    def share_all_h(l, carry):
         def one(j, carry):
-            rows = pl.ds(pl.multiple_of(j * MB_ROWS, MB_ROWS), MB_ROWS)
-            hx[p, j, me8] = hs[l, xl, rows, :]
-            dx[p, j, me8] = ds[l, c, rows, :]
-            for src in range(8):
-
-                @pl.when(src != me8)
-                def _(src=src):
-                    for ref, rs in ((hx, h_r), (dx, u_r)):
-                        block = ref.at[p, j, src]
-                        send(block, block, h_s.at[0, 0], rs.at[p, j, src], sibling).wait_recv()
-
-            acc[...] += lax.dot_general(
-                hx[p, j].reshape(8 * MB_ROWS, HALF),
-                dx[p, j].reshape(8 * MB_ROWS, HALF),
-                (((0,), (0,)), ((), ())),
-                preferred_element_type=jnp.float32,
-            )
-            return carry
-
-        lax.fori_loop(0, slots, one, 0)
-        gs[p] = acc[...].astype(jnp.bfloat16).reshape(4, 2, 64, HALF)
-        for_sums(p, lambda p, k, cc: gy(p, k, cc).start())
-        gr[p, c, 0] = gs[p, y, c]
-
-    def add_up(p, out):
-        for cs in range(2):
-
-            @pl.when(cs != c)
-            def _(cs=cs):
-                sum_wait(p, 0, cs).wait_recv()
-
-            for k in (1, 3, 2):
-                sum_wait(p, k, cs).wait_recv()
-            out[:, cs * HALF : (cs + 1) * HALF] = (
-                f32(gr[p, cs, 0]) + f32(gr[p, cs, 1]) + f32(gr[p, cs, 2]) + f32(gr[p, cs, 3])
-            )
-
-    def zr():
-        return send(zsend, zres, zr_s, zr_r, zpartner)
-
-    if FIRST_PAIR < 8:
-
-        @pl.when(pair)
-        def _():
-            collect(1 - own_p)
-
-    collect(own_p)
-    if FIRST_PAIR < 8:
-
-        @pl.when(pair)
-        def _():
-            add_up(1 - own_p, zsend)
-            zr().start()
-
-    add_up(own_p, gw_out.at[0])
-    if FIRST_PAIR < 8:
-
-        @pl.when(pair)
-        def _():
-            zr().wait_recv()
-            gw_out[0] = gw_out[0] + zres[...]
-
-    full = gw_out[0]
-    per_row = jnp.sum(full * wv[...].astype(jnp.float32), axis=1, keepdims=True)
-    gg_out[...] = jnp.sum(jnp.where(eye, per_row, 0.0), axis=0, keepdims=True)
-    gw_out[0] = full * gain_col
-
-    if FIRST_PAIR < 8:
-
-        @pl.when(pair)
-        def _():
-            zx().wait_send()
-            zr().wait_send()
+            for t in range(2):
+                share_h(l, j, t).start()
+            return carry
+
+        return lax.fori_loop(0, slots, one, carry)
 
     def drain_gather(i, carry):
         p = (own_p + i) % planes
@@ -571,7 +457,194 @@
         d_own(p).wait_send()
         return carry
 
-    lax.fori_loop(0, planes, drain_gather, 0)
+    @pl.when(last)
+    def _():
+        lax.fori_loop(0, layers, turn, 0)
+
+    wait_above()
+    lax.fori_loop(0, slots, forward, 0)
+
+    @pl.when(jnp.logical_not(last))
+    def _():
+        lax.fori_loop(0, layers, share_all_h, 0)
+        lax.fori_loop(0, layers, turn, 0)
+
+    lax.fori_loop(0, layers, slopes, 0)
+
+    @pl.when(jnp.logical_not(last))
+    def _():
+        lax.fori_loop(0, planes, drain_gather, 0)
+
+    if FIRST_PAIR > 0:
+
+        @pl.when(single)
+        def _():
+            hand_over(0)
+
+    def backward_layers(j, top, bottom):
+        rows = pl.ds(pl.multiple_of(j * MB_ROWS, MB_ROWS), MB_ROWS)
+        delta = cot[j]
+        for l in range(top, bottom - 1, -1):
+            df = f32(delta)
+            grad = (df * sl[l, j]).astype(jnp.bfloat16)
+            for q in range(4):
+                ds[l, q, rows, :] = grad[:, q * WIDE : (q + 1) * WIDE]
+            a = jnp.dot(grad, wt[l], preferred_element_type=jnp.float32)
+            r = rinv[l, j][:, 0:1]
+            xr = f32(xs[l, j]) * r
+            delta = (df + r * (a - xr * jnp.mean(a * xr, axis=-1, keepdims=True))).astype(jnp.bfloat16)
+        return delta
+
+    def backward(j, carry):
+        @pl.when(last)
+        def _():
+            rows_in(down_cot, cot, j, 0).wait()
+
+        @pl.when(jnp.logical_not(last))
+        def _():
+            bx_wait(j).wait_recv()
+
+        if FIRST_PAIR < 8:
+
+            @pl.when(jnp.logical_and(pair, jnp.logical_not(first)))
+            def _():
+                do[j] = backward_layers(j, 3, 0)
+                bx(j).start()
+
+        if FIRST_PAIR > 0:
+
+            @pl.when(jnp.logical_and(single, jnp.logical_not(first)))
+            def _():
+                do[j] = backward_layers(j, 1, 0)
+                bx(j).start()
+
+        @pl.when(first)
+        def _():
+            rows = pl.ds(pl.multiple_of(j * MB_ROWS, MB_ROWS), MB_ROWS)
+            delta = backward_layers(j, 1 if FIRST_PAIR > 0 else 3, 1)
+            grad = (f32(delta) * sl[0, j]).astype(jnp.bfloat16)
+            for q in range(4):
+                ds[0, q, rows, :] = grad[:, q * WIDE : (q + 1) * WIDE]
+
+        @pl.when(first)
+        def _():
+            share_all_u(j)
+
+        return carry
+
+    def share_all_u(j):
+        def one(l, carry):
+            for_owners(l, lambda t, cc: share_u(l, j, t, cc).start())
+            return carry
+
+        lax.fori_loop(0, layers, one, 0)
+
+    lax.fori_loop(0, slots, backward, 0)
+
+    @pl.when(jnp.logical_not(first))
+    def _():
+        lax.fori_loop(0, slots, lambda j, carry: (share_all_u(j), carry)[1], 0)
+
+    @pl.when(last)
+    def _():
+        lax.fori_loop(0, layers, share_all_h, 0)
+
+    def gy(p, k, t, cc):
+        to_y = (y + k) % 4
+        return send(
+            gs.at[p, to_y, t, cc], gr.at[p, quarter, k], g_s.at[p, k, 2 * t + cc], g_r.at[p, quarter, k],
+            at(2 * xh + t, to_y, z, cc),
+        )
+
+    def for_sums(p, act):
+        for k in (2, 1, 3, 0):
+            for t in range(2):
+                for cc in range(2):
+                    if k == 0:
+
+                        @pl.when(2 * t + cc != quarter)
+                        def _(k=k, t=t, cc=cc):
+                            act(p, k, t, cc)
+
+                    else:
+                        act(p, k, t, cc)
+
+    def sum_wait(p, k, q):
+        return send(gr.at[p, q, k], gr.at[p, q, k], g_s.at[p, k, q], g_r.at[p, q, k], sibling)
+
+    def collect(p):
+        l = 2 * p + xh
+        acc[...] = jnp.zeros_like(acc)
+
+        def all_h(j, carry):
+            hx[p, j, me8] = hs[l, mb_rows(j), :]
+            dx[p, j, me8] = ds[l, quarter, mb_rows(j), :]
+            for ax in range(4):
+                block = hx.at[p, j, 2 * ax + other]
+                send(block, block, h_s.at[0, 0], h_r.at[p, j, 2 * ax + other], sibling).wait_recv()
+            return carry
+
+        def one(j, carry):
+            for src in range(8):
+
+                @pl.when(src != me8)
+                def _(src=src):
+                    block = dx.at[p, j, src]
+                    send(block, block, u_s.at[0, 0], u_r.at[p, j, src], sibling).wait_recv()
+
+            acc[...] += lax.dot_general(
+                hx[p, j].reshape(8 * MB_ROWS, D),
+                dx[p, j].reshape(8 * MB_ROWS, WIDE),
+                (((0,), (0,)), ((), ())),
+                preferred_element_type=jnp.float32,
+            )
+            return carry
+
+        lax.fori_loop(0, slots, all_h, 0)
+        lax.fori_loop(0, slots, one, 0)
+        gs[p] = acc[...].astype(jnp.bfloat16).reshape(4, 2, 2, 64, WIDE)
+        for_sums(p, lambda p, k, t, cc: gy(p, k, t, cc).start())
+        gr[p, quarter, 0] = gs[p, y, xl, c]
+
+    def add_up(p, out):
+        for q in range(4):
+            for k in K:
+                sum_wait(p, k, q).wait_recv()
+
+            @pl.when(q != quarter)
+            def _(q=q):
+                sum_wait(p, 0, q).wait_recv()
+
+            out[:, q * WIDE : (q + 1) * WIDE] = f32(gr[p, q, 0]) + f32(gr[p, q, 1]) + f32(gr[p, q, 2]) + f32(gr[p, q, 3])
+
+    def zr():
+        return send(zsend, zres, zr_s, zr_r, zpartner)
+
+    if FIRST_PAIR < 8:
+
+        @pl.when(pair)
+        def _():
+            hand_over(1 - own_p)
+            hand_over(own_p)
+            collect(1 - own_p)
+
+    collect(own_p)
+    if FIRST_PAIR < 8:
+
+        @pl.when(pair)
+        def _():
+            add_up(1 - own_p, zsend)
+            zr().start()
+
+    if FIRST_PAIR < 8:
+
+        @pl.when(pair)
+        def _():
+            zx().wait_send()
+
+    @pl.when(last)
+    def _():
+        lax.fori_loop(0, planes, drain_gather, 0)
 
     def drain_relay(j, carry):
         @pl.when(jnp.logical_not(last))
@@ -588,7 +661,8 @@
 
     def drain_layers(l, carry):
         def drain_rows(j, carry):
-            for_owners(l, lambda t, cc: share_h(l, j, t, cc).wait_send())
+            for t in range(2):
+                share_h(l, j, t).wait_send()
             for_owners(l, lambda t, cc: share_u(l, j, t, cc).wait_send())
             return carry
 
@@ -596,9 +670,33 @@
 
     lax.fori_loop(0, layers, drain_layers, 0)
 
+    def drain_hand(p, carry):
+        def one(j, carry):
+            for k in K:
+                hand_h(p, j, k).wait_send()
+            return carry
+
+        return lax.fori_loop(0, slots, one, carry)
+
+    lax.fori_loop(0, planes, drain_hand, 0)
+
     def drain_sums(p, carry):
-        for_sums(p, lambda p, k, cc: gy(p, k, cc).wait_send())
-        return carry
+        for_sums(p, lambda p, k, t, cc: gy(p, k, t, cc).wait_send())
+        return carry
+
+    add_up(own_p, gw_out.at[0])
+    if FIRST_PAIR < 8:
+
+        @pl.when(pair)
+        def _():
+            zr().wait_recv()
+            gw_out[0] = gw_out[0] + zres[...]
+            zr().wait_send()
+
+    full = gw_out[0]
+    per_row = jnp.sum(full * wv[...].astype(jnp.float32), axis=1, keepdims=True)
+    gg_out[...] = jnp.sum(jnp.where(eye, per_row, 0.0), axis=0, keepdims=True)
+    gw_out[0] = full * gain_col
 
     lax.fori_loop(0, planes, drain_sums, 0)
 
@@ -612,19 +710,18 @@
         pltpu.VMEM((64, D), bf),
         pltpu.VMEM((nl, 4, 2, 2, 64, D), bf),
         pltpu.VMEM((nl, D, D), bf),
-        pltpu.VMEM((nl, 2, 4 * MB_ROWS, HALF), bf),
-        pltpu.VMEM((nl, 2, 4 * MB_ROWS, HALF), bf),
-        pltpu.VMEM((np_, 4, 8, MB_ROWS, HALF), bf),
-        pltpu.VMEM((np_, 4, 8, MB_ROWS, HALF), bf),
-        pltpu.VMEM((HALF, HALF), f4),
-        pltpu.VMEM((np_, 4, 2, 64, HALF), bf),
-        pltpu.VMEM((np_, 2, 4, 64, HALF), bf),
+        pltpu.VMEM((nl, 4 * MB_ROWS, D), bf),
+        pltpu.VMEM((nl, 4, 4 * MB_ROWS, D // 4), bf),
+        pltpu.VMEM((np_, 4, 8, MB_ROWS, D), bf),
+        pltpu.VMEM((np_, 4, 8, MB_ROWS, D // 4), bf),
+        pltpu.VMEM((D, D // 4), f4),
+        pltpu.VMEM((np_, 4, 2, 2, 64, D // 4), bf),
+        pltpu.VMEM((np_, 4, 4, 64, D // 4), bf),
         pltpu.VMEM((64, D), f4),
         pltpu.VMEM((64, D), f4),
-        pltpu.VMEM((nl, 4, MB_ROWS, D), bf),
+        pltpu.VMEM((nl + 1, 4, MB_ROWS, D), bf),
         pltpu.VMEM((nl, 4, MB_ROWS, D), f4),
         pltpu.VMEM((nl, 4, MB_ROWS, 128), f4),
-        pltpu.VMEM((4, MB_ROWS, D), bf),
         pltpu.VMEM((4, MB_ROWS, D), bf),
         pltpu.VMEM((4, MB_ROWS, D), bf),
         dma, dma,
@@ -633,8 +730,8 @@
         dma((np_, 4, 2)), dma((np_, 4, 2)), dma((np_, 4, 2)), dma((np_, 4, 2)),
         dma((np_, 39)), dma((np_,)),
         dma((4,)), dma((4,)), dma((4,)), dma((4,)),
-        dma((8, 4)), dma((np_, 4, 8)), dma((8, 4)), dma((np_, 4, 8)),
-        dma((np_, 4, 2)), dma((np_, 2, 4)),
+        dma((8, 2)), dma((np_, 4, 8)), dma((np_, 4, 3)), dma((8, 4)), dma((np_, 4, 8)),
+        dma((np_, 4, 4)), dma((np_, 4, 4)),
         dma, dma,
         pltpu.SemaphoreType.REGULAR((2,)),
         dma, dma((4,)),

time: 109 us -> 105 us (0.963)
  Pallas kernels: 106 us -> 102 us
    pallas_call x1, Pallas kernels: 106 us -> 102 us  [shards(): pl.pallas_call(kernel, out_shape=(jax.ShapeDtypeStruct((1, 64, D), f4), j...]
where the time goes in v6:
time: 105 us
  Pallas kernels  102 us (97%)
  local copies, waits for them, and re-layouts  2.19 us (2%)
    pallas_call x1, Pallas kernels, shards(): pl.pallas_call(kernel, out_shape=(jax.ShapeDtypeStruct((1, 64, D), f4), j...  102 us
    unnamed x4, local copies, waits for them, and re-layouts  2.19 us

profile of v6, /device:TPU:1, one launch (start us, length us, event | category | flops | bytes accessed | tf_op | source)
XLA Modules:
  0.0 104.6 jit_solution(2749638239349257350)
XLA Ops:
  0.6 101.8 %shard_map.77 = (f32[1,64,1024]{2,1,0:T(8,128)}, f32[1,64]{1,0:T(1,128)}) custom-call(bf16[2,64,1024]{2,1,0:T(8,128)(2,1)} %down_in.1, bf16[2,64,1024]{2,1,0:T(8,128)(2,1)} %up_in.1, bf16[2,64,1024]{2,1,0:T(8,128)(2,1)} %down_cot.1, bf16[2,64,1024]{2,1,0:T(8,128)(2,1)} %up_cot.1, bf16[1,64,1024]{2,1,0:T(8,128)(2,1)} %w_in.1, bf16[1,64]{1,0:T(2,128)(2,1)} %g_in.1), custom_call_target="tpu_custom_call" | custom-call | tf_op jit(solution)/shard_map/pallas_call | solution.py:740
  102.4 0.0 copy-start
  102.4 1.7 %copy.10 = f32[1,64,1024]{2,1,0:T(8,128)} copy(f32[1,64,1024]{2,1,0:T(8,128)} %get-tuple-element.4) | data formatting | bytes 524288
  104.1 0.0 copy-done
  104.1 0.5 copy.11
Async XLA Ops:
  102.4 1.7 %copy-start = (f32[1,64]{1,0:T(1,128)S(1)}, f32[1,64]{1,0:T(1,128)}, u32[]{:S(2)}) copy-start(f32[1,64]{1,0:T(1,128)} %get-tuple-element.5) | copy-start | bytes 772

commit v7 on v6

--- a/solution.py
+++ b/solution.py
@@ -421,12 +421,14 @@
 
         return carry
 
+    def slope(u):
+        u2 = u * u
+        t = jnp.tanh(SLOPE * (u + CUBIC * u2 * u))
+        return 0.5 * (1.0 + t) + 0.5 * u * (1.0 - t * t) * SLOPE * (1.0 + 3.0 * CUBIC * u2)
+
     def slopes(l, carry):
         def one(j, carry):
-            u = sl[l, j]
-            u2 = u * u
-            t = jnp.tanh(SLOPE * (u + CUBIC * u2 * u))
-            sl[l, j] = 0.5 * (1.0 + t) + 0.5 * u * (1.0 - t * t) * SLOPE * (1.0 + 3.0 * CUBIC * u2)
+            sl[l, j] = slope(sl[l, j])
             return carry
 
         return lax.fori_loop(0, slots, one, carry)
@@ -469,10 +471,9 @@
         lax.fori_loop(0, layers, share_all_h, 0)
         lax.fori_loop(0, layers, turn, 0)
 
-    lax.fori_loop(0, layers, slopes, 0)
-
     @pl.when(jnp.logical_not(last))
     def _():
+        lax.fori_loop(0, layers, slopes, 0)
         lax.fori_loop(0, planes, drain_gather, 0)
 
     if FIRST_PAIR > 0:
@@ -481,12 +482,12 @@
         def _():
             hand_over(0)
 
-    def backward_layers(j, top, bottom):
+    def backward_layers(j, top, bottom, fresh=False):
         rows = pl.ds(pl.multiple_of(j * MB_ROWS, MB_ROWS), MB_ROWS)
         delta = cot[j]
         for l in range(top, bottom - 1, -1):
             df = f32(delta)
-            grad = (df * sl[l, j]).astype(jnp.bfloat16)
+            grad = (df * (slope(sl[l, j]) if fresh else sl[l, j])).astype(jnp.bfloat16)
             for q in range(4):
                 ds[l, q, rows, :] = grad[:, q * WIDE : (q + 1) * WIDE]
             a = jnp.dot(grad, wt[l], preferred_element_type=jnp.float32)
@@ -506,9 +507,16 @@
 
         if FIRST_PAIR < 8:
 
-            @pl.when(jnp.logical_and(pair, jnp.logical_not(first)))
+            @pl.when(last)
+            def _():
+                do[j] = backward_layers(j, 3, 0, fresh=True)
+
+            @pl.when(jnp.logical_and(pair, jnp.logical_not(jnp.logical_or(first, last))))
             def _():
                 do[j] = backward_layers(j, 3, 0)
+
+            @pl.when(pair)
+            def _():
                 bx(j).start()
 
         if FIRST_PAIR > 0:

time: 105 us -> 104 us (level)
    pallas_call x1, Pallas kernels: 102 us -> 101 us  [shards(): pl.pallas_call(kernel, out_shape=(jax.ShapeDtypeStruct((1, 64, D), f4), j...]
where the time goes in v7:
time: 104 us; the launch traced here: 103 us
  Pallas kernels  101 us (97%)
  local copies, waits for them, and re-layouts  2.19 us (2%)
    pallas_call x1, Pallas kernels, shards(): pl.pallas_call(kernel, out_shape=(jax.ShapeDtypeStruct((1, 64, D), f4), j...  101 us
    unnamed x4, local copies, waits for them, and re-layouts  2.19 us

profile of v7, /device:TPU:1, one launch (start us, length us, event | category | flops | bytes accessed | tf_op | source)
XLA Modules:
  0.0 103.5 jit_solution(962677721486273303)
XLA Ops:
  0.6 100.7 %shard_map.77 = (f32[1,64,1024]{2,1,0:T(8,128)}, f32[1,64]{1,0:T(1,128)}) custom-call(bf16[2,64,1024]{2,1,0:T(8,128)(2,1)} %down_in.1, bf16[2,64,1024]{2,1,0:T(8,128)(2,1)} %up_in.1, bf16[2,64,1024]{2,1,0:T(8,128)(2,1)} %down_cot.1, bf16[2,64,1024]{2,1,0:T(8,128)(2,1)} %up_cot.1, bf16[1,64,1024]{2,1,0:T(8,128)(2,1)} %w_in.1, bf16[1,64]{1,0:T(2,128)(2,1)} %g_in.1), custom_call_target="tpu_custom_call" | custom-call | tf_op jit(solution)/shard_map/pallas_call | solution.py:748
  101.3 0.0 copy-start
  101.3 1.7 %copy.10 = f32[1,64,1024]{2,1,0:T(8,128)} copy(f32[1,64,1024]{2,1,0:T(8,128)} %get-tuple-element.4) | data formatting | bytes 524288
  103.0 0.0 copy-done
  103.0 0.5 copy.11
Async XLA Ops:
  101.3 1.7 %copy-start = (f32[1,64]{1,0:T(1,128)S(1)}, f32[1,64]{1,0:T(1,128)}, u32[]{:S(2)}) copy-start(f32[1,64]{1,0:T(1,128)} %get-tuple-element.5) | copy-start | bytes 772

commit v8 on v7

--- a/solution.py
+++ b/solution.py
@@ -39,8 +39,8 @@
     def ydev(k):
         return at(x, (y + k) % 4, z, c)
 
-    def zdev(k):
-        return at(x, y, (z + 8 + k) % 8, other)
+    def zdev(k, core):
+        return at(x, y, (z + 8 + k) % 8, core)
 
     sibling = at(x, y, z, other)
     pair = z >= FIRST_PAIR
@@ -68,7 +68,8 @@
 
         @pl.when(z + k < 8)
         def _(k=k):
-            pl.semaphore_signal(barrier, inc=1, device_id=zdev(k), device_id_type=MESH)
+            for core in (c, other):
+                pl.semaphore_signal(barrier, inc=1, device_id=zdev(k, core), device_id_type=MESH)
 
     if FIRST_PAIR < 8:
 
@@ -81,7 +82,7 @@
 
             @pl.when(z + k < 8)
             def _(k=k):
-                pl.semaphore_wait(above.at[k - 1], 1)
+                pl.semaphore_wait(above.at[k - 1], 2)
 
     def send(src, dst, ss, rs, to):
         return pltpu.make_async_remote_copy(
@@ -92,12 +93,13 @@
     gain_col = jnp.sum(jnp.where(eye, g_in[...].astype(jnp.float32), 0.0), axis=1, keepdims=True)
     load_w.wait()
     w[own_l, y, xl, c] = (wv[...].astype(jnp.float32) * gain_col).astype(jnp.bfloat16)
-    pl.semaphore_wait(barrier, len(peers) + jnp.minimum(z, 2) + ispair)
+    pl.semaphore_wait(barrier, len(peers) + 2 * jnp.minimum(z, 2) + ispair)
     for k in (1, 2):
 
         @pl.when(z >= k)
         def _(k=k):
-            pl.semaphore_signal(above.at[k - 1], inc=1, device_id=zdev(-k), device_id_type=MESH)
+            for core in (c, other):
+                pl.semaphore_signal(above.at[k - 1], inc=1, device_id=zdev(-k, core), device_id_type=MESH)
 
 
     A, B, ALL = pl.ds(0, HALF), pl.ds(HALF, HALF), pl.ds(0, D)
@@ -295,27 +297,24 @@
     lax.fori_loop(0, planes, gather_end, 0)
     lax.fori_loop(0, planes, gather_wait, 0)
 
-    if FIRST_PAIR == 8:
-
-        def f_route(j):
-            return zdev(1), j
-
-        def b_route(j):
-            return zdev(-1), j
-
-    else:
-        to_pair = (z == FIRST_PAIR - 1).astype(jnp.int32)
-        from_pair = ((z // 2) * 2 == FIRST_PAIR).astype(jnp.int32)
-
-        def f_route(j):
-            step = ispair * 2 + (1 - ispair) * (1 + to_pair * (j % 2))
-            slot = j - to_pair * (j - j // 2)
-            return zdev(step), slot
-
-        def b_route(j):
-            step = ispair * (2 + from_pair * (odd - 1)) + (1 - ispair)
-            slot = j + from_pair * (j + odd)
-            return zdev(-step), slot
+    def changes(*planes_below):
+        hit = sum((z == low).astype(jnp.int32) for low in planes_below)
+        return c + hit * (1 - 2 * c)
+
+    up_core = changes(0, 2, 3)
+    down_core = changes(1, 4, 5)
+    to_pair = (z == FIRST_PAIR - 1).astype(jnp.int32)
+    from_pair = ((z // 2) * 2 == FIRST_PAIR).astype(jnp.int32)
+
+    def f_route(j):
+        step = ispair * 2 + (1 - ispair) * (1 + to_pair * (j % 2))
+        slot = j - to_pair * (j - j // 2)
+        return zdev(step, up_core), slot
+
+    def b_route(j):
+        step = ispair * (2 + from_pair * (odd - 1)) + (1 - ispair)
+        slot = j + from_pair * (j + odd)
+        return zdev(-step, down_core), slot
 
     def fx(j):
         to, slot = f_route(j)

time: 104 us -> 103 us (level)
  Pallas kernels: 101 us -> 99.9 us
where the time goes in v8:
time: 103 us
  Pallas kernels  99.9 us (97%)
  local copies, waits for them, and re-layouts  2.19 us (2%)
    pallas_call x1, Pallas kernels, shards(): pl.pallas_call(kernel, out_shape=(jax.ShapeDtypeStruct((1, 64, D), f4), j...  99.9 us
    unnamed x4, local copies, waits for them, and re-layouts  2.19 us

profile of v8, /device:TPU:1, one launch (start us, length us, event | category | flops | bytes accessed | tf_op | source)
XLA Modules:
  0.0 102.8 jit_solution(3898980316177149207)
XLA Ops:
  0.6 99.9 %shard_map.77 = (f32[1,64,1024]{2,1,0:T(8,128)}, f32[1,64]{1,0:T(1,128)}) custom-call(bf16[2,64,1024]{2,1,0:T(8,128)(2,1)} %down_in.1, bf16[2,64,1024]{2,1,0:T(8,128)(2,1)} %up_in.1, bf16[2,64,1024]{2,1,0:T(8,128)(2,1)} %down_cot.1, bf16[2,64,1024]{2,1,0:T(8,128)(2,1)} %up_cot.1, bf16[1,64,1024]{2,1,0:T(8,128)(2,1)} %w_in.1, bf16[1,64]{1,0:T(2,128)(2,1)} %g_in.1), custom_call_target="tpu_custom_call" | custom-call | tf_op jit(solution)/shard_map/pallas_call | solution.py:747
  100.6 0.0 copy-start
  100.6 1.7 %copy.10 = f32[1,64,1024]{2,1,0:T(8,128)} copy(f32[1,64,1024]{2,1,0:T(8,128)} %get-tuple-element.4) | data formatting | bytes 524288
  102.2 0.0 copy-done
  102.2 0.5 copy.11
Async XLA Ops:
  100.6 1.7 %copy-start = (f32[1,64]{1,0:T(1,128)S(1)}, f32[1,64]{1,0:T(1,128)}, u32[]{:S(2)}) copy-start(f32[1,64]{1,0:T(1,128)} %get-tuple-element.5) | copy-start | bytes 772

commit v9 on v8

--- a/solution.py
+++ b/solution.py
@@ -414,10 +414,7 @@
             def _():
                 forward_layers(j, 4)
 
-        @pl.when(jnp.logical_not(last))
-        def _():
-            fx(j).start()
-
+        fx(j).start()
         return carry
 
     def slope(u):
@@ -463,7 +460,9 @@
         lax.fori_loop(0, layers, turn, 0)
 
     wait_above()
-    lax.fori_loop(0, slots, forward, 0)
+    @pl.when(jnp.logical_not(last))
+    def _():
+        lax.fori_loop(0, slots, forward, 0)
 
     @pl.when(jnp.logical_not(last))
     def _():
@@ -496,26 +495,13 @@
         return delta
 
     def backward(j, carry):
-        @pl.when(last)
-        def _():
-            rows_in(down_cot, cot, j, 0).wait()
-
-        @pl.when(jnp.logical_not(last))
-        def _():
-            bx_wait(j).wait_recv()
+        bx_wait(j).wait_recv()
 
         if FIRST_PAIR < 8:
 
-            @pl.when(last)
-            def _():
-                do[j] = backward_layers(j, 3, 0, fresh=True)
-
-            @pl.when(jnp.logical_and(pair, jnp.logical_not(jnp.logical_or(first, last))))
+            @pl.when(jnp.logical_and(pair, jnp.logical_not(first)))
             def _():
                 do[j] = backward_layers(j, 3, 0)
-
-            @pl.when(pair)
-            def _():
                 bx(j).start()
 
         if FIRST_PAIR > 0:
@@ -546,7 +532,21 @@
 
         lax.fori_loop(0, layers, one, 0)
 
-    lax.fori_loop(0, slots, backward, 0)
+    @pl.when(jnp.logical_not(last))
+    def _():
+        lax.fori_loop(0, slots, backward, 0)
+
+    def turn_round(j, carry):
+        fx_wait(j).wait_recv()
+        forward_layers(j, 4)
+        rows_in(down_cot, cot, j, 0).wait()
+        do[j] = backward_layers(j, 3, 0, fresh=True)
+        bx(j).start()
+        return carry
+
+    @pl.when(last)
+    def _():
+        lax.fori_loop(0, slots, turn_round, 0)
 
     @pl.when(jnp.logical_not(first))
     def _():

time: 103 us -> 102 us (level)
  no operation moved by 1% of the time
where the time goes in v9:
time: 102 us
  Pallas kernels  99 us (97%)
  local copies, waits for them, and re-layouts  2.19 us (2%)
    pallas_call x1, Pallas kernels, shards(): pl.pallas_call(kernel, out_shape=(jax.ShapeDtypeStruct((1, 64, D), f4), j...  99 us
    unnamed x4, local copies, waits for them, and re-layouts  2.19 us

profile of v9, /device:TPU:1, one launch (start us, length us, event | category | flops | bytes accessed | tf_op | source)
XLA Modules:
  0.0 101.9 jit_solution(2106906129490069483)
XLA Ops:
  0.6 99.0 %shard_map.77 = (f32[1,64,1024]{2,1,0:T(8,128)}, f32[1,64]{1,0:T(1,128)}) custom-call(bf16[2,64,1024]{2,1,0:T(8,128)(2,1)} %down_in.1, bf16[2,64,1024]{2,1,0:T(8,128)(2,1)} %up_in.1, bf16[2,64,1024]{2,1,0:T(8,128)(2,1)} %down_cot.1, bf16[2,64,1024]{2,1,0:T(8,128)(2,1)} %up_cot.1, bf16[1,64,1024]{2,1,0:T(8,128)(2,1)} %w_in.1, bf16[1,64]{1,0:T(2,128)(2,1)} %g_in.1), custom_call_target="tpu_custom_call" | custom-call | tf_op jit(solution)/shard_map/pallas_call | solution.py:747
  99.7 0.0 copy-start
  99.7 1.7 %copy.10 = f32[1,64,1024]{2,1,0:T(8,128)} copy(f32[1,64,1024]{2,1,0:T(8,128)} %get-tuple-element.4) | data formatting | bytes 524288
  101.3 0.0 copy-done
  101.3 0.5 copy.11
Async XLA Ops:
  99.7 1.7 %copy-start = (f32[1,64]{1,0:T(1,128)S(1)}, f32[1,64]{1,0:T(1,128)}, u32[]{:S(2)}) copy-start(f32[1,64]{1,0:T(1,128)} %get-tuple-element.5) | copy-start | bytes 772
